TPU v7x, 32 devices: a whole 2x2x4 slice. The times are simulated.
32 devices in a mesh: dp: 8 (over y, x, core), mp: 4 (over z).
Axes of the slice: x: 2, y: 2, z: 4, core: 2. Of those that a mesh axis runs over, the one named last changes fastest.
Arguments:
- tokens: bfloat16 [4, 3136, 768], P(None, ('dp', 'mp')), may hold values from -6 to 6
- cotangent: bfloat16 [4, 3136, 768], P(None, ('dp', 'mp')), may hold values from -6 to 6
- clip_adapter: int32 [4], replicated, may hold values from 0 to 7
- gain_one: float32 [768], replicated, may hold values from 0.1 to 1.9
- gain_two: float32 [768], replicated, may hold values from 0.1 to 1.9
- w_qkv: bfloat16 [768, 3, 768], P('dp', None, 'mp'), may hold values from -0.21875 to 0.21875
- w_out: bfloat16 [768, 768], P('mp', 'dp'), may hold values from -1.75 to 1.75
- w_up: bfloat16 [768, 3072], P('dp', 'mp'), may hold values from -0.21875 to 0.21875
- w_down: bfloat16 [3072, 768], P('mp', 'dp'), may hold values from -0.109375 to 0.109375
- adapters: float32 [128, 12288], P(None, ('dp', 'mp'))
- moment_one: float32 [128, 12288], P(None, ('dp', 'mp')), may hold values from -128 to 128
- moment_two: float32 [128, 12288], P(None, ('dp', 'mp')), may hold values from 392 to 1568
Outputs:
- activations: bfloat16 [4, 3136, 768], P(None, ('dp', 'mp'))
- input_grad: bfloat16 [4, 3136, 768], P(None, ('dp', 'mp'))
- adapter_grad: float32 [128, 12288], P(None, ('dp', 'mp'))
- new_adapters: float32 [128, 12288], P(None, ('dp', 'mp'))
- new_moment_one: float32 [128, 12288], P(None, ('dp', 'mp'))
- new_moment_two: float32 [128, 12288], P(None, ('dp', 'mp'))
- adapter_copy: bfloat16 [128, 12288], P(None, ('dp', 'mp'))
All inputs are finite; a program needn't handle non-finite values.
Results may differ from a plain program's by a relative error of at most 0.017.
Values may be sent and summed in bfloat16 or wider, within the bound.
A program may use at most 192 MiB of HBM per device.

v0:
```python
import math

import jax
import jax.numpy as jnp
from jax import lax
from jax.sharding import PartitionSpec as P

HEAD = 64
FRAME = 196
RANK = 16
CLIP_FRAMES = 16
STEP = 5


norm_epsilon = 1e-06
beta_first = 0.5
beta_second = 0.5
learn_rate = 0.05
weight_decay = 0.01
adam_epsilon = 1e-08
highest = lax.Precision.HIGHEST


def product(left_side, right_side):
    return jnp.dot(left_side, right_side, precision=highest, preferred_element_type=jnp.float32)


def plain_dot(left_side, right_side):
    return jnp.dot(left_side, right_side, preferred_element_type=jnp.float32)


def against(left_side, right_side):
    return lax.dot_general(
        left_side, right_side, (((1,), (1,)), ((), ())), preferred_element_type=jnp.float32
    )


def across(left_side, right_side):
    return lax.dot_general(
        left_side,
        right_side,
        (((0,), (0,)), ((), ())),
        precision=highest,
        preferred_element_type=jnp.float32,
    )


def normalize(values_in, gain):
    center = values_in - jnp.mean(values_in, axis=-1, keepdims=True)
    spread = jnp.mean(center * center, axis=-1, keepdims=True)
    return center * lax.rsqrt(spread + norm_epsilon) * gain


def shards(
    tokens,
    cotangent,
    clip_adapter,
    gain_one,
    gain_two,
    w_qkv,
    w_out,
    w_up,
    w_down,
    adapters,
    moment_one,
    moment_two,
):
    groups = lax.axis_size("mp")
    member = lax.axis_index("mp")
    group_index = lax.axis_index("dp")
    micro_count, shard_rows, model_width = tokens.shape
    local_width = w_out.shape[0]
    unit_count = w_up.shape[1]
    hidden_width = unit_count * groups
    head_count = local_width // HEAD
    rank_all = adapters.shape[0]
    full_width = adapters.shape[1] * lax.axis_size(("dp", "mp"))
    group_rows = shard_rows * groups
    frames = group_rows // FRAME
    frames_micro = frames * lax.axis_size("dp")
    score_scale = 1.0 / math.sqrt(HEAD)
    shape_heads = (frames, FRAME, head_count, HEAD)
    frozen = (
        lax.all_gather(w_qkv, "dp", axis=0, tiled=True),
        lax.all_gather(w_out, "dp", axis=1, tiled=True),
        lax.all_gather(w_up, "dp", axis=0, tiled=True),
        lax.all_gather(w_down, "dp", axis=1, tiled=True),
    )
    adapt_all = lax.all_gather(adapters.astype(jnp.bfloat16), ("dp", "mp"), axis=1, tiled=True)
    qkv_all = frozen[0].reshape(model_width, 3 * local_width)
    out_all = frozen[1]
    up_all = frozen[2]
    down_all = frozen[3]
    grad_sum = jnp.zeros((rank_all, full_width), jnp.float32)
    outputs = []
    input_grads = []

    def placed(piece_grad, span, offset):
        return lax.dynamic_update_slice_in_dim(
            jnp.zeros((RANK, span), jnp.float32), piece_grad, offset, 1
        )

    for micro_index in range(micro_count):
        first_frame = micro_index * frames_micro + group_index * frames
        chosen = lax.dynamic_index_in_dim(
            clip_adapter, first_frame // CLIP_FRAMES, 0, keepdims=False
        )
        mine = lax.dynamic_slice_in_dim(adapt_all, chosen * RANK, RANK, 0)
        inputs = tokens[micro_index].astype(jnp.float32)
        normed_one = normalize(inputs, gain_one).astype(jnp.bfloat16)
        a_qkv = mine[:, 0:model_width]
        b_qkv = jnp.concatenate(
            [
                lax.dynamic_slice_in_dim(
                    mine, (1 + section) * model_width + member * local_width, local_width, 1
                )
                for section in range(3)
            ],
            axis=1,
        )
        a_out = lax.dynamic_slice_in_dim(
            mine, 4 * model_width + member * local_width, local_width, 1
        )
        b_out = mine[:, 5 * model_width : 6 * model_width]
        a_up = mine[:, 6 * model_width : 7 * model_width]
        b_up = lax.dynamic_slice_in_dim(mine, 7 * model_width + member * unit_count, unit_count, 1)
        a_down = lax.dynamic_slice_in_dim(
            mine, 7 * model_width + hidden_width + member * unit_count, unit_count, 1
        )
        b_down = mine[:, 7 * model_width + 2 * hidden_width :]
        b_qkv_float = b_qkv.astype(jnp.float32)
        b_out_float = b_out.astype(jnp.float32)
        b_up_float = b_up.astype(jnp.float32)
        b_down_float = b_down.astype(jnp.float32)
        rows_one = lax.all_gather(normed_one, "mp", axis=0, tiled=True)
        low_qkv = against(rows_one, a_qkv)
        projected = (plain_dot(rows_one, qkv_all) + product(low_qkv, b_qkv_float)).astype(
            jnp.bfloat16
        )
        queries = projected[:, 0:local_width].reshape(shape_heads)
        key_rows = projected[:, local_width : 2 * local_width].reshape(shape_heads)
        value_rows = projected[:, 2 * local_width :].reshape(shape_heads)
        scores = (
            jnp.einsum("fqhd,fkhd->fhqk", queries, key_rows, preferred_element_type=jnp.float32)
            * score_scale
        )
        row_max = jnp.max(scores, axis=-1, keepdims=True)
        exponent = jnp.exp(scores - row_max)
        row_total = jnp.sum(exponent, axis=-1, keepdims=True)
        soft_weights = exponent / row_total
        log_total = row_max + jnp.log(row_total)
        attended = jnp.einsum(
            "fhqk,fkhd->fqhd",
            soft_weights.astype(jnp.bfloat16),
            value_rows,
            preferred_element_type=jnp.float32,
        )
        attended = attended.reshape(group_rows, local_width).astype(jnp.bfloat16)
        low_out = against(attended, a_out)
        middle = inputs + lax.psum_scatter(
            plain_dot(attended, out_all) + product(low_out, b_out_float),
            "mp",
            scatter_dimension=0,
            tiled=True,
        )
        normed_two = normalize(middle, gain_two).astype(jnp.bfloat16)
        rows_two = lax.all_gather(normed_two, "mp", axis=0, tiled=True)
        low_up = against(rows_two, a_up)
        hidden = plain_dot(rows_two, up_all) + product(low_up, b_up_float)
        active = jax.nn.gelu(hidden, approximate=False).astype(jnp.bfloat16)
        low_down = against(active, a_down)
        outputs.append(
            (
                middle
                + lax.psum_scatter(
                    (plain_dot(active, down_all) + product(low_down, b_down_float)).astype(
                        jnp.bfloat16
                    ),
                    "mp",
                    scatter_dimension=0,
                    tiled=True,
                ).astype(jnp.float32)
            ).astype(jnp.bfloat16)
        )
        grad_rows = lax.all_gather(cotangent[micro_index], "mp", axis=0, tiled=True)
        grad_float = grad_rows.astype(jnp.float32)
        through_down = product(grad_float, b_down_float.T)
        grad_active = against(grad_rows, down_all) + product(
            through_down, a_down.astype(jnp.float32)
        )
        grad_b_down = across(low_down, grad_float)
        grad_a_down = across(through_down, active.astype(jnp.float32))
        unused_value, gelu_pull = jax.vjp(
            lambda pre_values: jax.nn.gelu(pre_values, approximate=False), hidden
        )
        grad_hidden = gelu_pull(grad_active)[0].astype(jnp.bfloat16)
        hidden_float = grad_hidden.astype(jnp.float32)
        grad_b_up = across(low_up, hidden_float)
        through_up = product(hidden_float, b_up_float.T)
        grad_a_up = across(through_up, rows_two.astype(jnp.float32))
        a_up_float = a_up.astype(jnp.float32)
        grad_normed_two = lax.psum_scatter(
            against(grad_hidden, up_all) + product(through_up, a_up_float),
            "mp",
            scatter_dimension=0,
            tiled=True,
        )
        unused_two, norm_pull_two = jax.vjp(
            lambda values_in: normalize(values_in, gain_two), middle
        )
        grad_middle = cotangent[micro_index].astype(jnp.float32) + norm_pull_two(grad_normed_two)[0]
        branch_rows = lax.all_gather(grad_middle.astype(jnp.bfloat16), "mp", axis=0, tiled=True)
        branch_float = branch_rows.astype(jnp.float32)
        through_out = product(branch_float, b_out_float.T)
        grad_attended = (
            against(branch_rows, out_all) + product(through_out, a_out.astype(jnp.float32))
        ).astype(jnp.bfloat16)
        grad_b_out = across(low_out, branch_float)
        grad_a_out = across(through_out, attended.astype(jnp.float32))
        grad_heads = grad_attended.reshape(shape_heads)
        scores_again = (
            jnp.einsum("fqhd,fkhd->fhqk", queries, key_rows, preferred_element_type=jnp.float32)
            * score_scale
        )
        soft_again = jnp.exp(scores_again - log_total)
        grad_values = jnp.einsum(
            "fhqk,fqhd->fkhd",
            soft_again.astype(jnp.bfloat16),
            grad_heads,
            preferred_element_type=jnp.float32,
        )
        grad_soft = jnp.einsum(
            "fqhd,fkhd->fhqk", grad_heads, value_rows, preferred_element_type=jnp.float32
        )
        inner = jnp.sum(soft_again * grad_soft, axis=-1, keepdims=True)
        grad_scores = (soft_again * (grad_soft - inner)).astype(jnp.bfloat16)
        grad_queries = (
            jnp.einsum("fhqk,fkhd->fqhd", grad_scores, key_rows, preferred_element_type=jnp.float32)
            * score_scale
        )
        grad_keys = (
            jnp.einsum("fhqk,fqhd->fkhd", grad_scores, queries, preferred_element_type=jnp.float32)
            * score_scale
        )
        grad_projected = jnp.concatenate(
            [
                grad_queries.reshape(group_rows, local_width),
                grad_keys.reshape(group_rows, local_width),
                grad_values.reshape(group_rows, local_width),
            ],
            axis=1,
        ).astype(jnp.bfloat16)
        projected_float = grad_projected.astype(jnp.float32)
        grad_b_qkv = across(low_qkv, projected_float)
        through_qkv = product(projected_float, b_qkv_float.T)
        grad_a_qkv = across(through_qkv, rows_one.astype(jnp.float32))
        a_qkv_float = a_qkv.astype(jnp.float32)
        grad_normed_one = lax.psum_scatter(
            (against(grad_projected, qkv_all) + product(through_qkv, a_qkv_float)).astype(
                jnp.bfloat16
            ),
            "mp",
            scatter_dimension=0,
            tiled=True,
        ).astype(jnp.float32)
        unused_one, norm_pull_one = jax.vjp(
            lambda values_in: normalize(values_in, gain_one), inputs
        )
        input_grads.append((grad_middle + norm_pull_one(grad_normed_one)[0]).astype(jnp.bfloat16))
        rows_grad = jnp.concatenate(
            [
                grad_a_qkv,
                placed(grad_b_qkv[:, 0:local_width], model_width, member * local_width),
                placed(
                    grad_b_qkv[:, local_width : 2 * local_width], model_width, member * local_width
                ),
                placed(grad_b_qkv[:, 2 * local_width :], model_width, member * local_width),
                placed(grad_a_out, model_width, member * local_width),
                grad_b_out,
                grad_a_up,
                placed(grad_b_up, hidden_width, member * unit_count),
                placed(grad_a_down, hidden_width, member * unit_count),
                grad_b_down,
            ],
            axis=1,
        )
        grad_sum = grad_sum + lax.dynamic_update_slice_in_dim(
            jnp.zeros((rank_all, full_width), jnp.float32), rows_grad, chosen * RANK, 0
        )
    owner_grad = lax.psum_scatter(grad_sum, ("dp", "mp"), scatter_dimension=1, tiled=True)
    first_moment = beta_first * moment_one + (1.0 - beta_first) * owner_grad
    second_moment = beta_second * moment_two + (1.0 - beta_second) * owner_grad * owner_grad
    first_hat = first_moment / (1.0 - beta_first**STEP)
    second_hat = second_moment / (1.0 - beta_second**STEP)
    updated = adapters - learn_rate * (
        first_hat / (jnp.sqrt(second_hat) + adam_epsilon) + weight_decay * adapters
    )
    return (
        jnp.stack(outputs),
        jnp.stack(input_grads),
        owner_grad,
        updated,
        first_moment,
        second_moment,
        updated.astype(jnp.bfloat16),
    )


def solution(mesh):
    return jax.shard_map(
        shards,
        mesh=mesh,
        in_specs=(
            P(None, ("dp", "mp"), None),
            P(None, ("dp", "mp"), None),
            P(),
            P(),
            P(),
            P("dp", None, "mp"),
            P("mp", "dp"),
            P("dp", "mp"),
            P("mp", "dp"),
            P(None, ("dp", "mp")),
            P(None, ("dp", "mp")),
            P(None, ("dp", "mp")),
        ),
        out_specs=(
            P(None, ("dp", "mp"), None),
            P(None, ("dp", "mp"), None),
            P(None, ("dp", "mp")),
            P(None, ("dp", "mp")),
            P(None, ("dp", "mp")),
            P(None, ("dp", "mp")),
            P(None, ("dp", "mp")),
        ),
        check_vma=False,
    )
```

profile of v0, /device:TPU:0, one launch (start us, length us, event | category | flops | bytes accessed | tf_op | source)
XLA Modules:
  0.0 1052.1 jit_solution(7568669672368673360)
XLA Ops:
  18.4 20.9 %all-gather.4 = bf16[4,98,768]{2,1,0:T(8,128)(2,1)S(1)} all-gather(bf16[1,98,768]{2,1,0:T(8,128)(2,1)S(1)} %get-tuple-element.166), channel_id=1, replica_groups=mesh['dp'=8,'mp'=4] {'mp'}, dimensions={0}, use_global_device_ids=true | all-gather | bytes 752640 | tf_op jit(solution)/shard_map/all_gather | solution.py:135
  39.8 15.9 %all_gather.64 = bf16[768,3,192]{2,1,0:T(4,128)(2,1)} all-gather(bf16[96,3,192]{2,1,0:T(4,128)(2,1)S(1)} %copy.258), channel_id=1, replica_groups=mesh['dp'=8,'mp'=4] {'dp'}, dimensions={0}, use_global_device_ids=true | all-gather | bytes 995328 | tf_op jit(solution)/shard_map/all_gather | solution.py:84
  55.7 2.6 copy.259
  58.4 10.1 all_gather.66
  68.5 18.5 %all-gather.6 = bf16[4,98,768]{2,1,0:T(8,128)(2,1)} all-gather(bf16[1,98,768]{2,1,0:T(8,128)(2,1)S(1)} %get-tuple-element.169), channel_id=1, replica_groups=mesh['dp'=8,'mp'=4] {'mp'}, dimensions={0}, use_global_device_ids=true | all-gather | bytes 752640 | tf_op jit(solution)/shard_map/all_gather | solution.py:135
  88.3 17.4 %all-gather.8 = bf16[4,98,768]{2,1,0:T(8,128)(2,1)} all-gather(bf16[1,98,768]{2,1,0:T(8,128)(2,1)S(1)} %get-tuple-element.167), channel_id=1, replica_groups=mesh['dp'=8,'mp'=4] {'mp'}, dimensions={0}, use_global_device_ids=true | all-gather | bytes 752640 | tf_op jit(solution)/shard_map/all_gather | solution.py:135
  107.8 17.4 %all-gather.10 = bf16[4,98,768]{2,1,0:T(8,128)(2,1)} all-gather(bf16[1,98,768]{2,1,0:T(8,128)(2,1)S(1)} %get-tuple-element.168), channel_id=1, replica_groups=mesh['dp'=8,'mp'=4] {'mp'}, dimensions={0}, use_global_device_ids=true | all-gather | bytes 752640 | tf_op jit(solution)/shard_map/all_gather | solution.py:135
  127.2 3.7 fusion.363
  131.7 21.6 %all-gather.1 = bf16[1,392,768]{2,0,1:T(2,128)(2,1)} all-gather(bf16[1,98,768]{2,0,1:T(2,128)(2,1)S(1)} %get-tuple-element.126), channel_id=3, replica_groups=mesh['dp'=8,'mp'=4] {'mp'}, dimensions={1}, use_global_device_ids=true | all-gather | bytes 752640 | tf_op jit(solution)/shard_map/all_gather | solution.py:185
  153.3 23.0 %all-gather.2 = bf16[1,392,768]{2,0,1:T(2,128)(2,1)} all-gather(bf16[1,98,768]{2,0,1:T(2,128)(2,1)S(1)} %get-tuple-element.127), channel_id=4, replica_groups=mesh['dp'=8,'mp'=4] {'mp'}, dimensions={1}, use_global_device_ids=true | all-gather | bytes 752640 | tf_op jit(solution)/shard_map/all_gather | solution.py:185
  176.3 22.1 %all-gather.3 = bf16[1,392,768]{2,0,1:T(2,128)(2,1)} all-gather(bf16[1,98,768]{2,0,1:T(2,128)(2,1)S(1)} %get-tuple-element.129), channel_id=5, replica_groups=mesh['dp'=8,'mp'=4] {'mp'}, dimensions={1}, use_global_device_ids=true | all-gather | bytes 752640 | tf_op jit(solution)/shard_map/all_gather | solution.py:185
  198.4 18.2 %all-gather = bf16[1,392,768]{2,0,1:T(2,128)(2,1)} all-gather(bf16[1,98,768]{2,0,1:T(2,128)(2,1)S(1)} %copy-done.84), channel_id=2, replica_groups=mesh['dp'=8,'mp'=4] {'mp'}, dimensions={1}, use_global_device_ids=true | all-gather | bytes 752640 | tf_op jit(solution)/shard_map/all_gather | solution.py:185
  284.8 76.5 %fusion.342 = (f32[104,768]{1,0:T(8,128)}, f32[104,768]{1,0:T(8,128)}, f32[104,768]{1,0:T(8,128)}, f32[104,768]{1,0:T(8,128)S(1)}) fusion(f32[392,768]{1,0:T(8,128)} %convolution_add_fusion.14, f32[392,768]{1,0:T(8,128)} %convolution_add_fusion.17, f32[392,768]{1,0:T(8,128)} %convolution_add_fusion.20, f32[392,768]{1,0:T(8,128)} %convolution_add_fusion.23), kind=kCustom, calls=%all-reduce-scatter.17 | all-reduce-scatter fusion | flops 1277953 | bytes 6095360
  362.3 2.6 collective-permute-start.2
  368.1 2.7 fusion.269
  370.8 2.5 fusion.261
  374.4 2.6 fusion.253
  378.0 2.6 fusion.277
  385.6 3.4 collective-permute-start.6
  400.1 3.2 concatenate.58
  406.0 3.2 concatenate.52
  413.0 17.4 %all-gather.7 = bf16[4,98,768]{2,1,0:T(8,128)(2,1)} all-gather(bf16[1,98,768]{2,1,0:T(8,128)(2,1)S(1)} %get-tuple-element.165), channel_id=1, replica_groups=mesh['dp'=8,'mp'=4] {'mp'}, dimensions={0}, use_global_device_ids=true | all-gather | bytes 752640 | tf_op jit(solution)/shard_map/all_gather | solution.py:167
  432.4 16.4 %all-gather.9 = bf16[4,98,768]{2,1,0:T(8,128)(2,1)} all-gather(bf16[1,98,768]{2,1,0:T(8,128)(2,1)} %get-tuple-element.164), channel_id=1, replica_groups=mesh['dp'=8,'mp'=4] {'mp'}, dimensions={0}, use_global_device_ids=true | all-gather | bytes 752640 | tf_op jit(solution)/shard_map/all_gather | solution.py:167
  450.9 19.8 %all-gather.11 = bf16[4,98,768]{2,1,0:T(8,128)(2,1)} all-gather(bf16[1,98,768]{2,1,0:T(8,128)(2,1)} %get-tuple-element.163), channel_id=1, replica_groups=mesh['dp'=8,'mp'=4] {'mp'}, dimensions={0}, use_global_device_ids=true | all-gather | bytes 752640 | tf_op jit(solution)/shard_map/all_gather | solution.py:167
  472.8 16.3 %all-gather.5 = bf16[4,98,768]{2,1,0:T(8,128)(2,1)} all-gather(bf16[1,98,768]{2,1,0:T(8,128)(2,1)} %get-tuple-element.162), channel_id=1, replica_groups=mesh['dp'=8,'mp'=4] {'mp'}, dimensions={0}, use_global_device_ids=true | all-gather | bytes 752640 | tf_op jit(solution)/shard_map/all_gather | solution.py:167
  493.1 2.5 fusion.275
  495.7 6.3 multiply_convert_fusion.6
  502.0 3.6 add_convert_fusion.2
  513.2 4.2 multiply_convert_fusion.5
  525.9 4.4 multiply_convert_fusion.4
  538.8 4.2 multiply_convert_fusion.7
  548.9 69.6 %fusion.341 = (f32[104,768]{1,0:T(8,128)}, f32[104,768]{1,0:T(8,128)}, f32[104,768]{1,0:T(8,128)}, f32[104,768]{1,0:T(8,128)}) fusion(f32[392,768]{1,0:T(8,128)} %convolution_add_fusion.10, f32[392,768]{1,0:T(8,128)} %convolution_add_fusion.1, f32[392,768]{1,0:T(8,128)} %convolution_add_fusion.4, f32[392,768]{1,0:T(8,128)} %convolution_add_fusion.7), kind=kCustom, calls=%all-reduce-scatter.16 | all-reduce-scatter fusion | flops 1277953 | bytes 6095360
  619.5 4.4 collective-permute-start.10
  628.9 3.2 collective-permute-start.14
  654.1 3.2 concatenate.62
  657.4 3.3 concatenate.64
  660.6 3.2 concatenate.66
  663.9 3.2 concatenate.60
  670.7 15.9 %all-gather.15 = bf16[4,98,768]{2,1,0:T(8,128)(2,1)} all-gather(bf16[1,98,768]{2,1,0:T(8,128)(2,1)S(1)} %fusion.173), channel_id=1, replica_groups=mesh['dp'=8,'mp'=4] {'mp'}, dimensions={0}, use_global_device_ids=true | all-gather | bytes 752640 | tf_op jit(solution)/shard_map/all_gather | solution.py:212
  719.6 16.0 %all-gather.14 = bf16[4,98,768]{2,1,0:T(8,128)(2,1)} all-gather(bf16[1,98,768]{2,1,0:T(8,128)(2,1)S(1)} %fusion.174), channel_id=1, replica_groups=mesh['dp'=8,'mp'=4] {'mp'}, dimensions={0}, use_global_device_ids=true | all-gather | bytes 752640 | tf_op jit(solution)/shard_map/all_gather | solution.py:212
  765.2 15.9 %all-gather.13 = bf16[4,98,768]{2,1,0:T(8,128)(2,1)} all-gather(bf16[1,98,768]{2,1,0:T(8,128)(2,1)S(1)} %fusion.175), channel_id=1, replica_groups=mesh['dp'=8,'mp'=4] {'mp'}, dimensions={0}, use_global_device_ids=true | all-gather | bytes 752640 | tf_op jit(solution)/shard_map/all_gather | solution.py:212
  810.4 16.0 %all-gather.12 = bf16[4,98,768]{2,1,0:T(8,128)(2,1)} all-gather(bf16[1,98,768]{2,1,0:T(8,128)(2,1)S(1)} %fusion.176), channel_id=1, replica_groups=mesh['dp'=8,'mp'=4] {'mp'}, dimensions={0}, use_global_device_ids=true | all-gather | bytes 752640 | tf_op jit(solution)/shard_map/all_gather | solution.py:212
  889.6 3.3 broadcast.444
  902.3 2.9 fusion.17
  920.2 89.2 %fusion.343 = (bf16[104,768]{1,0:T(8,128)(2,1)S(1)}, bf16[104,768]{1,0:T(8,128)(2,1)S(1)}, bf16[104,768]{1,0:T(8,128)(2,1)S(1)}, bf16[104,768]{1,0:T(8,128)(2,1)...) fusion(bf16[392,768]{1,0:T(8,128)(2,1)} %fusion.19, ...), kind=kCustom, calls=%all-reduce-scatter.18 | all-reduce-scatter fusion | flops 2555905 | bytes 6095360
  1009.5 4.5 collective-permute-start.11
  1015.0 2.5 collective-permute-start.13
  1018.3 2.9 collective-permute-start.15
  (1090 shorter events, 384.4 us)
Async XLA Ops:
  7.2 210.7 %all-gather.20.cloned.1.call-start = ((), (), s32[]{:S(2)}) async-start(), calls=%async_computation.1 | async-start | bytes 3244032 | tf_op jit(solution)/shard_map/all_gather | solution.py:89
  8.9 486.8 %all-gather.22.cloned.1.call-start = ((), (), s32[]{:S(2)}) async-start(), calls=%async_computation.2 | async-start | bytes 1327104 | tf_op jit(solution)/shard_map/all_gather | solution.py:86
  9.6 492.4 %all-gather.24.cloned.1.call-start = ((), (), s32[]{:S(2)}) async-start(), calls=%async_computation.3 | async-start | bytes 1327104 | tf_op jit(solution)/shard_map/all_gather | solution.py:87
  10.4 1032.8 %reduce-scatter.34.cloned.1.call-start = ((), (), s32[]{:S(2)}) async-start(), calls=%async_computation.4 | async-start | bytes 6488064 | tf_op jit(solution)/shard_map/reduce_scatter | solution.py:290
  15.5 378.4 %copy-start.32 = (bf16[1,98,768]{2,1,0:T(8,128)(2,1)}, bf16[1,98,768]{2,1,0:T(8,128)(2,1)S(1)}, u32[]{:S(2)}) copy-start(bf16[1,98,768]{2,1,0:T(8,128)(2,1)S(1)} %get-tuple-element.109) | copy-start | bytes 451588
  16.3 23.0 %copy-start.34 = (bf16[1,98,768]{2,1,0:T(8,128)(2,1)}, bf16[1,98,768]{2,1,0:T(8,128)(2,1)S(1)}, u32[]{:S(2)}) copy-start(bf16[1,98,768]{2,1,0:T(8,128)(2,1)S(1)} %get-tuple-element.195) | copy-start | bytes 451588
  16.3 387.0 %copy-start.30 = (bf16[1,98,768]{2,1,0:T(8,128)(2,1)}, bf16[1,98,768]{2,1,0:T(8,128)(2,1)S(1)}, u32[]{:S(2)}) copy-start(bf16[1,98,768]{2,1,0:T(8,128)(2,1)S(1)} %get-tuple-element.113) | copy-start | bytes 451588
  16.3 23.0 %copy-start.258 = (f32[98]{0:T(128)}, f32[98]{0:T(128)S(1)}, u32[]{:S(2)}) copy-start(f32[98]{0:T(128)S(1)} %broadcast_multiply_fusion.1) | copy-start | bytes 1180
  17.1 22.2 %copy-start.277 = (f32[98]{0:T(128)}, f32[98]{0:T(128)S(1)}, u32[]{:S(2)}) copy-start(f32[98]{0:T(128)S(1)} %fusion.319) | copy-start | bytes 1180
  17.1 22.2 %copy-start.262 = (f32[98]{0:T(128)}, f32[98]{0:T(128)S(1)}, u32[]{:S(2)}) copy-start(f32[98]{0:T(128)S(1)} %broadcast_multiply_fusion.3) | copy-start | bytes 1180
  39.6 181.8 %copy-start.14 = (bf16[392,768]{1,0:T(8,128)(2,1)}, bf16[392,768]{1,0:T(8,128)(2,1)S(1)}, u32[]{:S(2)}) copy-start(bf16[392,768]{1,0:T(8,128)(2,1)S(1)} %reshape.409) | copy-start | bytes 1806340
  88.3 145.4 %copy-start.16 = (bf16[392,768]{1,0:T(8,128)(2,1)}, bf16[392,768]{1,0:T(8,128)(2,1)S(1)}, u32[]{:S(2)}) copy-start(bf16[392,768]{1,0:T(8,128)(2,1)S(1)} %reshape.413) | copy-start | bytes 1806340
  131.0 45.3 %copy-start.78 = (bf16[1,98,768]{2,0,1:T(2,128)(2,1)}, bf16[1,98,768]{2,0,1:T(2,128)(2,1)S(1)}, u32[]{:S(2)}) copy-start(bf16[1,98,768]{2,0,1:T(2,128)(2,1)S(1)} %get-tuple-element.127) | copy-start | bytes 451588
  131.0 45.3 %copy-start.75 = (bf16[1,98,768]{2,0,1:T(2,128)(2,1)}, bf16[1,98,768]{2,0,1:T(2,128)(2,1)S(1)}, u32[]{:S(2)}) copy-start(bf16[1,98,768]{2,0,1:T(2,128)(2,1)S(1)} %get-tuple-element.129) | copy-start | bytes 451588
  153.3 45.1 %copy-start.84 = (bf16[1,98,768]{2,0,1:T(2,128)(2,1)S(1)}, bf16[1,98,768]{2,0,1:T(2,128)(2,1)}, u32[]{:S(2)}) copy-start(bf16[1,98,768]{2,0,1:T(2,128)(2,1)} %get-tuple-element.128) | copy-start | bytes 451588
  176.3 40.3 %copy-start.317 = (u32[32]{0:T(128)S(1)}, u32[32]{0:T(128)}, u32[]{:S(2)}) copy-start(u32[32]{0:T(128)} %constant.465) | copy-start | bytes 388
  220.6 31.8 %copy-start.239 = (bf16[16,192]{1,0:T(8,128)(2,1)}, bf16[16,192]{1,0:T(8,128)(2,1)S(1)}, u32[]{:S(2)}) copy-start(bf16[16,192]{1,0:T(8,128)(2,1)S(1)} %get-tuple-element.118) | copy-start | bytes 18436
  220.6 31.8 %copy-start.241 = (bf16[16,192]{1,0:T(8,128)(2,1)}, bf16[16,192]{1,0:T(8,128)(2,1)S(1)}, u32[]{:S(2)}) copy-start(bf16[16,192]{1,0:T(8,128)(2,1)S(1)} %get-tuple-element.119) | copy-start | bytes 18436
  220.6 31.8 %copy-start.243 = (bf16[16,192]{1,0:T(8,128)(2,1)}, bf16[16,192]{1,0:T(8,128)(2,1)S(1)}, u32[]{:S(2)}) copy-start(bf16[16,192]{1,0:T(8,128)(2,1)S(1)} %get-tuple-element.120) | copy-start | bytes 18436
  361.4 27.7 %copy-start.127 = (f32[104,768]{1,0:T(8,128)}, f32[104,768]{1,0:T(8,128)S(1)}, u32[]{:S(2)}) copy-start(f32[104,768]{1,0:T(8,128)S(1)} %get-tuple-element.61) | copy-start | bytes 958468
  362.3 29.3 %collective-permute-start.2 = (f32[18,768]{1,0:T(8,128)S(1)}, f32[18,768]{1,0:T(8,128)S(1)}, u32[]{:S(2)}, u32[]{:S(2)}) collective-permute-start(f32[18,768]{1,0:T(8,128)S(1)} %slice.222), channel_id=1, source_target_pairs={{0,1},{1,2},{2,3},{4,5},{5,6},{6,7},{8,9},{9,10},{10,11},{12,13},{... | collective-permute-start | bytes 165896
  382.2 13.7 %collective-permute-start.4 = (f32[18,768]{1,0:T(8,128)}, f32[18,768]{1,0:T(8,128)S(1)}, u32[]{:S(2)}, u32[]{:S(2)}) collective-permute-start(f32[18,768]{1,0:T(8,128)} %slice.224), channel_id=1, source_target_pairs={{0,1},{1,2},{2,3},{4,5},{5,6},{6,7},{8,9},{9,10},{10,11},{12,13},{... | collective-permute-start | bytes 165896
  385.6 14.5 %collective-permute-start.6 = (f32[18,768]{1,0:T(8,128)}, f32[18,768]{1,0:T(8,128)}, u32[]{:S(2)}, u32[]{:S(2)}) collective-permute-start(f32[18,768]{1,0:T(8,128)} %slice.226), channel_id=1, source_target_pairs={{0,1},{1,2},{2,3},{4,5},{5,6},{6,7},{8,9},{9,10},{10,11},{12,13},{... | collective-permute-start | bytes 165896
  389.7 16.4 %collective-permute-start = (f32[18,768]{1,0:T(8,128)}, f32[18,768]{1,0:T(8,128)}, u32[]{:S(2)}, u32[]{:S(2)}) collective-permute-start(f32[18,768]{1,0:T(8,128)} %slice.220), channel_id=1, source_target_pairs={{0,1},{1,2},{2,3},{4,5},{5,6},{6,7},{8,9},{9,10},{10,11},{12,13},{... | collective-permute-start | bytes 165896
  619.5 34.6 %collective-permute-start.10 = (f32[18,768]{1,0:T(8,128)S(1)}, f32[18,768]{1,0:T(8,128)}, u32[]{:S(2)}, u32[]{:S(2)}) collective-permute-start(f32[18,768]{1,0:T(8,128)S(1)} %slice.230), channel_id=1, source_target_pairs={{0,1},{1,2},{2,3},{4,5},{5,6},{6,7},{8,9},{9,10},{10,11},{12,13},{... | collective-permute-start | bytes 165896
  625.4 31.9 %collective-permute-start.12 = (f32[18,768]{1,0:T(8,128)}, f32[18,768]{1,0:T(8,128)}, u32[]{:S(2)}, u32[]{:S(2)}) collective-permute-start(f32[18,768]{1,0:T(8,128)} %slice.232), channel_id=1, source_target_pairs={{0,1},{1,2},{2,3},{4,5},{5,6},{6,7},{8,9},{9,10},{10,11},{12,13},{... | collective-permute-start | bytes 165896
  628.9 31.7 %collective-permute-start.14 = (f32[18,768]{1,0:T(8,128)}, f32[18,768]{1,0:T(8,128)}, u32[]{:S(2)}, u32[]{:S(2)}) collective-permute-start(f32[18,768]{1,0:T(8,128)} %slice.234), channel_id=1, source_target_pairs={{0,1},{1,2},{2,3},{4,5},{5,6},{6,7},{8,9},{9,10},{10,11},{12,13},{... | collective-permute-start | bytes 165896
  633.6 30.3 %collective-permute-start.8 = (f32[18,768]{1,0:T(8,128)}, f32[18,768]{1,0:T(8,128)}, u32[]{:S(2)}, u32[]{:S(2)}) collective-permute-start(f32[18,768]{1,0:T(8,128)} %slice.228), channel_id=1, source_target_pairs={{0,1},{1,2},{2,3},{4,5},{5,6},{6,7},{8,9},{9,10},{10,11},{12,13},{... | collective-permute-start | bytes 165896
  1009.5 25.8 %copy-start.139 = (bf16[104,768]{1,0:T(8,128)(2,1)}, bf16[104,768]{1,0:T(8,128)(2,1)S(1)}, u32[]{:S(2)}) copy-start(bf16[104,768]{1,0:T(8,128)(2,1)S(1)} %get-tuple-element.72) | copy-start | bytes 479236
  1009.5 25.2 %copy-start.143 = (bf16[104,768]{1,0:T(8,128)(2,1)S(1)}, bf16[104,768]{1,0:T(8,128)(2,1)}, u32[]{:S(2)}) copy-start(bf16[104,768]{1,0:T(8,128)(2,1)} %get-tuple-element.75) | copy-start | bytes 479236
  1009.5 25.8 %copy-start.142 = (bf16[104,768]{1,0:T(8,128)(2,1)S(1)}, bf16[104,768]{1,0:T(8,128)(2,1)}, u32[]{:S(2)}) copy-start(bf16[104,768]{1,0:T(8,128)(2,1)} %get-tuple-element.74) | copy-start | bytes 479236
  1009.5 26.1 %copy-start.31 = (bf16[1,98,768]{2,1,0:T(8,128)(2,1)S(1)}, bf16[1,98,768]{2,1,0:T(8,128)(2,1)}, u32[]{:S(2)}) copy-start(bf16[1,98,768]{2,1,0:T(8,128)(2,1)} %copy-done.30) | copy-start | bytes 451588
  1009.5 26.1 %copy-start.259 = (f32[98]{0:T(128)S(1)}, f32[98]{0:T(128)}, u32[]{:S(2)}) copy-start(f32[98]{0:T(128)} %copy-done.258) | copy-start | bytes 1180
  1009.5 17.2 %collective-permute-start.11 = (bf16[18,768]{1,0:T(8,128)(2,1)S(1)}, bf16[18,768]{1,0:T(8,128)(2,1)S(1)}, u32[]{:S(2)}, u32[]{:S(2)}) collective-permute-start(bf16[18,768]{1,0:T(8,128)(2,1)S(1)} %slice.231), channel_id=1, source_target_pairs={{0,1},{1,2},{2,3},{4,5},{5,6},{6,7},{8,9},{9,10},{10,11},{12,13},{... | collective-permute-start | bytes 82952
  1014.1 21.8 %copy-start.33 = (bf16[1,98,768]{2,1,0:T(8,128)(2,1)S(1)}, bf16[1,98,768]{2,1,0:T(8,128)(2,1)}, u32[]{:S(2)}) copy-start(bf16[1,98,768]{2,1,0:T(8,128)(2,1)} %copy-done.32) | copy-start | bytes 451588
  1014.1 21.8 %copy-start.35 = (bf16[1,98,768]{2,1,0:T(8,128)(2,1)S(1)}, bf16[1,98,768]{2,1,0:T(8,128)(2,1)}, u32[]{:S(2)}) copy-start(bf16[1,98,768]{2,1,0:T(8,128)(2,1)} %copy-done.34) | copy-start | bytes 451588
  1014.1 21.8 %copy-start.37 = (bf16[1,98,768]{2,1,0:T(8,128)(2,1)S(1)}, bf16[1,98,768]{2,1,0:T(8,128)(2,1)}, u32[]{:S(2)}) copy-start(bf16[1,98,768]{2,1,0:T(8,128)(2,1)} %copy-done.36) | copy-start | bytes 451588
  1014.1 21.8 %copy-start.261 = (f32[98]{0:T(128)S(1)}, f32[98]{0:T(128)}, u32[]{:S(2)}) copy-start(f32[98]{0:T(128)} %copy-done.260) | copy-start | bytes 1180
  1014.1 21.8 %copy-start.263 = (f32[98]{0:T(128)S(1)}, f32[98]{0:T(128)}, u32[]{:S(2)}) copy-start(f32[98]{0:T(128)} %copy-done.262) | copy-start | bytes 1180
  1014.1 21.8 %copy-start.265 = (f32[98]{0:T(128)S(1)}, f32[98]{0:T(128)}, u32[]{:S(2)}) copy-start(f32[98]{0:T(128)} %copy-done.264) | copy-start | bytes 1180
  1014.1 21.8 %copy-start.278 = (f32[98]{0:T(128)S(1)}, f32[98]{0:T(128)}, u32[]{:S(2)}) copy-start(f32[98]{0:T(128)} %copy-done.277) | copy-start | bytes 1180
  1015.0 14.7 %collective-permute-start.13 = (bf16[18,768]{1,0:T(8,128)(2,1)S(1)}, bf16[18,768]{1,0:T(8,128)(2,1)S(1)}, u32[]{:S(2)}, u32[]{:S(2)}) collective-permute-start(bf16[18,768]{1,0:T(8,128)(2,1)S(1)} %slice.233), channel_id=1, source_target_pairs={{0,1},{1,2},{2,3},{4,5},{5,6},{6,7},{8,9},{9,10},{10,11},{12,13},{... | collective-permute-start | bytes 82952
  1018.3 14.4 %collective-permute-start.15 = (bf16[18,768]{1,0:T(8,128)(2,1)S(1)}, bf16[18,768]{1,0:T(8,128)(2,1)S(1)}, u32[]{:S(2)}, u32[]{:S(2)}) collective-permute-start(bf16[18,768]{1,0:T(8,128)(2,1)S(1)} %slice.235), channel_id=1, source_target_pairs={{0,1},{1,2},{2,3},{4,5},{5,6},{6,7},{8,9},{9,10},{10,11},{12,13},{... | collective-permute-start | bytes 82952
  1022.0 13.3 %collective-permute-start.9 = (bf16[18,768]{1,0:T(8,128)(2,1)S(1)}, bf16[18,768]{1,0:T(8,128)(2,1)S(1)}, u32[]{:S(2)}, u32[]{:S(2)}) collective-permute-start(bf16[18,768]{1,0:T(8,128)(2,1)S(1)} %slice.229), channel_id=1, source_target_pairs={{0,1},{1,2},{2,3},{4,5},{5,6},{6,7},{8,9},{9,10},{10,11},{12,13},{... | collective-permute-start | bytes 82952
  1024.7 15.4 %collective-permute-start.1 = (bf16[18,768]{1,0:T(8,128)(2,1)S(1)}, bf16[18,768]{1,0:T(8,128)(2,1)S(1)}, u32[]{:S(2)}, u32[]{:S(2)}) collective-permute-start(bf16[18,768]{1,0:T(8,128)(2,1)S(1)} %slice.221), channel_id=1, source_target_pairs={{0,1},{1,2},{2,3},{4,5},{5,6},{6,7},{8,9},{9,10},{10,11},{12,13},{... | collective-permute-start | bytes 82952
  1026.7 13.7 %collective-permute-start.3 = (bf16[18,768]{1,0:T(8,128)(2,1)S(1)}, bf16[18,768]{1,0:T(8,128)(2,1)S(1)}, u32[]{:S(2)}, u32[]{:S(2)}) collective-permute-start(bf16[18,768]{1,0:T(8,128)(2,1)S(1)} %slice.223), channel_id=1, source_target_pairs={{0,1},{1,2},{2,3},{4,5},{5,6},{6,7},{8,9},{9,10},{10,11},{12,13},{... | collective-permute-start | bytes 82952
  1029.7 11.0 %collective-permute-start.5 = (bf16[18,768]{1,0:T(8,128)(2,1)S(1)}, bf16[18,768]{1,0:T(8,128)(2,1)S(1)}, u32[]{:S(2)}, u32[]{:S(2)}) collective-permute-start(bf16[18,768]{1,0:T(8,128)(2,1)S(1)} %slice.225), channel_id=1, source_target_pairs={{0,1},{1,2},{2,3},{4,5},{5,6},{6,7},{8,9},{9,10},{10,11},{12,13},{... | collective-permute-start | bytes 82952
  1032.8 8.2 collective-permute-start.7
  (290 other events, 1261.1 us)
Sparse Core Ops, SparseCore 0:
  11.5 66.6 all-gather.19
  80.1 22.4 all-gather.21
  104.4 24.0 all-gather.23
  900.8 126.2 reduce-scatter.33
where the time goes:
time: 1070 us; the launch traced here: 1050 us
  blocking collectives  554 us (52%)
  local copies, waits for them, and re-layouts  204 us (19%)
  matrix products  197 us (18%)
  starting transfers between devices  41.4 us (4%)
  other arithmetic  31.5 us (3%)
  between operations  22.1 us (2%)
    unnamed x3, blocking collectives  235 us
    unnamed x717, local copies, waits for them, and re-layouts  108 us
    all_gather x4, blocking collectives, shards(): grad_rows = lax.all_gather(cotangent[micro_index], 'mp', axis=0, tiled=True)  84.9 us
    all_gather x4, blocking collectives, shards(): rows_one = lax.all_gather(normed_one, 'mp', axis=0, tiled=True)  74.2 us
    dot_general x48, matrix products, product(): jnp.dot(left_side, right_side, precision=highest, preferred_element_type=...  70.2 us
    all_gather x4, blocking collectives, shards(): rows_two = lax.all_gather(normed_two, 'mp', axis=0, tiled=True)  69.9 us
    all_gather x4, blocking collectives, shards(): lax.all_gather(grad_middle.astype(jnp.bfloat16), 'mp', axis=0, tiled=True)  63.8 us
    dot_general x32, matrix products, against(): lax.dot_general(left_side, right_side, (((1,), (1,)), ((), ())), preferre...  42.5 us
  transfers between devices with their start and end apart: 20, of which 0 were waited for; matrix products, arithmetic and copies ran while one was open for 35% of the time, Pallas kernels for 0%

commit v1 on v0

v1 whole, which is shorter than its diff:
```python
import math

import jax
import jax.numpy as jnp
from jax import lax
from jax.sharding import PartitionSpec as P

HEAD = 64
FRAME = 196
RANK = 16
CLIP_FRAMES = 16
STEP = 5

norm_epsilon = 1e-06
beta_first = 0.5
beta_second = 0.5
learn_rate = 0.05
weight_decay = 0.01
adam_epsilon = 1e-08


def dot(left, right):
    return jnp.dot(left, right, preferred_element_type=jnp.float32)


def dot_t(left, right):
    return lax.dot_general(left, right, (((1,), (1,)), ((), ())), preferred_element_type=jnp.float32)


def t_dot(left, right):
    return lax.dot_general(left, right, (((0,), (0,)), ((), ())), preferred_element_type=jnp.float32)


def half(values):
    return values.astype(jnp.bfloat16)


def norm_parts(values):
    center = values - jnp.mean(values, axis=-1, keepdims=True)
    spread = jnp.mean(center * center, axis=-1, keepdims=True)
    inverse = lax.rsqrt(spread + norm_epsilon)
    return center * inverse, inverse


def norm_back(unit, inverse, gain, grad):
    scaled = grad * gain
    first = jnp.mean(scaled, axis=-1, keepdims=True)
    second = jnp.mean(scaled * unit, axis=-1, keepdims=True)
    return inverse * (scaled - first - unit * second)


def shards(
    tokens,
    cotangent,
    clip_adapter,
    gain_one,
    gain_two,
    w_qkv,
    w_out,
    w_up,
    w_down,
    adapters,
    moment_one,
    moment_two,
):
    groups = lax.axis_size("mp")
    member = lax.axis_index("mp")
    group_index = lax.axis_index("dp")
    micro_count, shard_rows, width = tokens.shape
    hidden_width = w_up.shape[1] * groups
    heads = width // HEAD
    rank_all = adapters.shape[0]
    full_width = adapters.shape[1] * lax.axis_size(("dp", "mp"))
    frames = shard_rows * groups // FRAME
    frames_micro = frames * lax.axis_size("dp")
    scale = 1.0 / math.sqrt(HEAD)
    span = FRAME // shard_rows
    mine = micro_count // span
    part = member % span
    pairs = [[first * span + k for k in range(span)] for first in range(groups // span)]

    def swap(rows):
        return lax.all_to_all(
            rows, "mp", split_axis=0, concat_axis=1, axis_index_groups=pairs, tiled=True
        ).reshape(mine * FRAME, width)

    def swap_back(rows):
        return lax.all_to_all(
            rows.reshape(mine, FRAME, width),
            "mp",
            split_axis=1,
            concat_axis=0,
            axis_index_groups=pairs,
            tiled=True,
        )

    inputs = swap(tokens).astype(jnp.float32)
    dy = swap(cotangent)

    def whole(weight, first, second):
        return lax.all_gather(
            lax.all_gather(weight, first[0], axis=first[1], tiled=True),
            second[0],
            axis=second[1],
            tiled=True,
        )

    qkv_all = whole(w_qkv, ("dp", 0), ("mp", 2)).reshape(width, 3 * width)
    out_all = whole(w_out, ("dp", 1), ("mp", 0))
    up_all = whole(w_up, ("dp", 0), ("mp", 1))
    down_all = whole(w_down, ("dp", 1), ("mp", 0))
    table = lax.all_gather(half(adapters), ("dp", "mp"), axis=1, tiled=True)
    table = table.reshape(rank_all // RANK, RANK, full_width)
    clips = jnp.stack(
        [
            ((part * mine + i) * frames_micro + group_index * frames + member // span)
            // CLIP_FRAMES
            for i in range(mine)
        ]
    )
    chosen = clip_adapter[clips]
    own = table[chosen].reshape(mine * RANK, full_width)
    ends = [0, width, 4 * width, 5 * width, 6 * width, 7 * width]
    ends += [7 * width + hidden_width, 7 * width + 2 * hidden_width, full_width]
    a_qkv, b_qkv, a_out, b_out, a_up, b_up, a_down, b_down = [
        own[:, ends[i] : ends[i + 1]] for i in range(8)
    ]
    rows = mine * FRAME
    row_frame = lax.broadcasted_iota(jnp.int32, (rows, mine * RANK), 0) // FRAME
    column_frame = lax.broadcasted_iota(jnp.int32, (rows, mine * RANK), 1) // RANK
    mask = row_frame == column_frame

    def low(values):
        return half(jnp.where(mask, values, 0.0))

    shape_heads = (mine, FRAME, heads, HEAD)
    unit_one, inverse_one = norm_parts(inputs)
    normed_one = half(unit_one * gain_one)
    low_qkv = low(dot_t(normed_one, a_qkv))
    projected = half(dot(normed_one, qkv_all) + dot(low_qkv, b_qkv))
    queries = projected[:, 0:width].reshape(shape_heads)
    keys = projected[:, width : 2 * width].reshape(shape_heads)
    values = projected[:, 2 * width :].reshape(shape_heads)
    scores = jnp.einsum("fqhd,fkhd->fhqk", queries, keys, preferred_element_type=jnp.float32)
    scores = scores * scale
    exponent = jnp.exp(scores - jnp.max(scores, axis=-1, keepdims=True))
    soft = exponent / jnp.sum(exponent, axis=-1, keepdims=True)
    soft_half = half(soft)
    attended = half(
        jnp.einsum("fhqk,fkhd->fqhd", soft_half, values, preferred_element_type=jnp.float32)
    ).reshape(rows, width)
    low_out = low(dot_t(attended, a_out))
    middle = inputs + dot(attended, out_all) + dot(low_out, b_out)
    unit_two, inverse_two = norm_parts(middle)
    normed_two = half(unit_two * gain_two)
    low_up = low(dot_t(normed_two, a_up))
    hidden = dot(normed_two, up_all) + dot(low_up, b_up)
    phi = 0.5 * (1.0 + lax.erf(hidden * math.sqrt(0.5)))
    active = half(hidden * phi)
    slope = phi + hidden * jnp.exp(-0.5 * hidden * hidden) * (1.0 / math.sqrt(2.0 * math.pi))
    low_down = low(dot_t(active, a_down))
    outputs = half(middle + dot(active, down_all) + dot(low_down, b_down))

    through_down = low(dot_t(dy, b_down))
    d_active = dot_t(dy, down_all) + dot(through_down, a_down)
    d_hidden = half(d_active * slope)
    through_up = low(dot_t(d_hidden, b_up))
    d_normed_two = dot_t(d_hidden, up_all) + dot(through_up, a_up)
    d_middle = dy.astype(jnp.float32) + norm_back(unit_two, inverse_two, gain_two, d_normed_two)
    d_branch = half(d_middle)
    through_out = low(dot_t(d_branch, b_out))
    d_attended = half(dot_t(d_branch, out_all) + dot(through_out, a_out))
    d_heads = d_attended.reshape(shape_heads)
    d_values = jnp.einsum("fhqk,fqhd->fkhd", soft_half, d_heads, preferred_element_type=jnp.float32)
    d_soft = jnp.einsum("fqhd,fkhd->fhqk", d_heads, values, preferred_element_type=jnp.float32)
    inner = jnp.sum(soft * d_soft, axis=-1, keepdims=True)
    d_scores = half(soft * (d_soft - inner))
    d_queries = scale * jnp.einsum(
        "fhqk,fkhd->fqhd", d_scores, keys, preferred_element_type=jnp.float32
    )
    d_keys = scale * jnp.einsum(
        "fhqk,fqhd->fkhd", d_scores, queries, preferred_element_type=jnp.float32
    )
    d_projected = half(
        jnp.concatenate([d.reshape(rows, width) for d in (d_queries, d_keys, d_values)], axis=1)
    )
    through_qkv = low(dot_t(d_projected, b_qkv))
    d_normed_one = dot_t(d_projected, qkv_all) + dot(through_qkv, a_qkv)
    input_grad = half(d_middle + norm_back(unit_one, inverse_one, gain_one, d_normed_one))
    grads = half(jnp.concatenate(
        [
            t_dot(through_qkv, normed_one),
            t_dot(low_qkv, d_projected),
            t_dot(through_out, attended),
            t_dot(low_out, d_branch),
            t_dot(through_up, normed_two),
            t_dot(low_up, d_hidden),
            t_dot(through_down, active),
            t_dot(low_down, dy),
        ],
        axis=1,
    ))
    pick = (
        lax.broadcasted_iota(jnp.int32, (rank_all, mine * RANK), 0)
        == jnp.repeat(chosen, RANK)[None, :] * RANK
        + lax.broadcasted_iota(jnp.int32, (rank_all, mine * RANK), 1) % RANK
    ).astype(jnp.bfloat16)
    owner_grad = lax.psum_scatter(
        dot(pick, grads), ("dp", "mp"), scatter_dimension=1, tiled=True
    )
    first_moment = beta_first * moment_one + (1.0 - beta_first) * owner_grad
    second_moment = beta_second * moment_two + (1.0 - beta_second) * owner_grad * owner_grad
    first_hat = first_moment / (1.0 - beta_first**STEP)
    second_hat = second_moment / (1.0 - beta_second**STEP)
    updated = adapters - learn_rate * (
        first_hat / (jnp.sqrt(second_hat) + adam_epsilon) + weight_decay * adapters
    )
    return (
        swap_back(outputs),
        swap_back(input_grad),
        owner_grad,
        updated,
        first_moment,
        second_moment,
        updated.astype(jnp.bfloat16),
    )


def solution(mesh):
    spread = P(None, ("dp", "mp"))
    rows = P(None, ("dp", "mp"), None)
    return jax.shard_map(
        shards,
        mesh=mesh,
        in_specs=(
            rows,
            rows,
            P(),
            P(),
            P(),
            P("dp", None, "mp"),
            P("mp", "dp"),
            P("dp", "mp"),
            P("mp", "dp"),
            spread,
            spread,
            spread,
        ),
        out_specs=(rows, rows, spread, spread, spread, spread, spread),
        check_vma=False,
    )
```

time: 1070 us -> 602 us (0.56); the launches traced: 1050 us -> 597 us
  blocking collectives: 554 us -> 25.6 us
  waiting for transfers between devices: 1.48 us -> 384 us
  local copies, waits for them, and re-layouts: 204 us -> 69.9 us
  matrix products: 197 us -> 77.2 us
  starting transfers between devices: 41.4 us -> 15.3 us
  other arithmetic: 31.5 us -> 9.93 us
    all_gather x18 -> x2, blocking collectives: 319 us -> 25.6 us  [whole(): lax.all_gather(weight, first[0], axis=first[1], tiled=True)]
    all_gather x3 -> x7, waiting for transfers between devices: 0.02 us -> 287 us  [the longest x4 228 us: whole(): lax.all_gather(lax.all_gather(weight, first[0], axis=first[1], tiled=True...]
    unnamed x3 -> x0, blocking collectives: 235 us -> none
    dot_general x152 -> x38, matrix products: 197 us -> 71.6 us  [the longest x13 36 us: dot(): return jnp.dot(left, right, preferred_element_type=jnp.float32)]
    unnamed x717 -> x94, local copies, waits for them, and re-layouts: 108 us -> 13.8 us
    reduce_scatter x1, waiting for transfers between devices: 0.01 us -> 77.8 us  [shards(): lax.psum_scatter(dot(pick, grads), ('dp', 'mp'), scatter_dimension=1, til...]
    unnamed x16 -> x0, starting transfers between devices: 41.3 us -> none
    all_to_all x0 -> x4, waiting for transfers between devices: none -> 17.1 us  [the longest x2 9.03 us: swap_back(): lax.all_to_all(rows.reshape(mine, FRAME, width), 'mp', split_axis=1, conc...]
  transfers between devices with their start and end apart: 20 -> 12, of which waited for: 0 -> 9; matrix products, arithmetic and copies ran while one was open for 35% -> 15% of each run, Pallas kernels for 0% -> 0%
where the time goes in v1:
time: 602 us; the launch traced here: 597 us
  waiting for transfers between devices  384 us (64%)
  matrix products  77.2 us (13%)
  local copies, waits for them, and re-layouts  69.9 us (12%)
  blocking collectives  25.6 us (4%)
  starting transfers between devices  15.3 us (3%)
  between operations  15.2 us (3%)
  other arithmetic  9.93 us (2%)
    all_gather x4, waiting for transfers between devices, whole(): lax.all_gather(lax.all_gather(weight, first[0], axis=first[1], tiled=True...  228 us
    reduce_scatter x1, waiting for transfers between devices, shards(): lax.psum_scatter(dot(pick, grads), ('dp', 'mp'), scatter_dimension=1, til...  77.8 us
    all_gather x1, waiting for transfers between devices, shards(): table = lax.all_gather(half(adapters), ('dp', 'mp'), axis=1, tiled=True)  54.2 us
    dot_general x13, matrix products, dot(): return jnp.dot(left, right, preferred_element_type=jnp.float32)  36 us
    all_gather x2, blocking collectives, whole(): lax.all_gather(weight, first[0], axis=first[1], tiled=True)  25.6 us
    dot_general x12, matrix products, dot_t(): lax.dot_general(left, right, (((1,), (1,)), ((), ())), preferred_element_...  21 us
    unnamed x94, local copies, waits for them, and re-layouts  13.8 us
  transfers between devices with their start and end apart: 12, of which 9 were waited for; matrix products, arithmetic and copies ran while one was open for 15% of the time, Pallas kernels for 0%

profile of v1, /device:TPU:0, one launch (start us, length us, event | category | flops | bytes accessed | tf_op | source)
XLA Modules:
  0.0 596.6 jit_solution(183410729237181733)
XLA Ops:
  9.8 16.1 %all_gather.27 = bf16[768,3,192]{2,1,0:T(4,128)(2,1)S(1)} all-gather(bf16[96,3,192]{2,1,0:T(4,128)(2,1)S(1)} %copy.124), channel_id=1, replica_groups=mesh['dp'=8,'mp'=4] {'dp'}, dimensions={0}, use_global_device_ids=true | all-gather | bytes 995328 | tf_op jit(solution)/shard_map/all_gather | solution.py:102
  25.9 2.1 copy.125
  28.9 9.5 %all_gather.30 = bf16[192,768]{0,1:T(8,128)(2,1)S(1)} all-gather(bf16[192,96]{0,1:T(8,128)(2,1)S(1)} %copy.134), channel_id=1, replica_groups=mesh['dp'=8,'mp'=4] {'dp'}, dimensions={1}, use_global_device_ids=true | all-gather | bytes 331776 | tf_op jit(solution)/shard_map/all_gather | solution.py:102
  40.8 3.5 all-to-all-start
  46.3 8.0 %all-to-all-done = bf16[4,98,768]{2,1,0:T(8,128)(2,1)S(1)} async-done(((bf16[4,98,768]{2,1,0:T(8,128)(2,1)}), bf16[4,98,768]{2,1,0:T(8,128)(2,1)S(1)}, u32[]{:S(2)}, u32[]{:S(2)}) %all-to-all-start) | async-done | bytes 602144 | tf_op jit(solution)/shard_map/all_to_all | solution.py:83
  54.3 4.2 all-to-all-start.2
  59.9 4.9 all-gather.18.cloned.1.call-done
  70.1 66.2 %all-gather.8.cloned.1.call-done = bf16[768,3,768]{0,2,1:T(8,128)(2,1)} async-done(((bf16[768,3,192]{0,2,1:T(8,128)(2,1)}), bf16[768,3,768]{0,2,1:T(8,128)(2,1)}) %all-gather.8.cloned.1.call-update) | async-done | bytes 3538960 | tf_op jit(solution)/shard_map/all_gather | solution.py:101
  136.4 5.6 fusion.81
  141.9 54.2 %all-gather.10.cloned.1.call-done = bf16[128,12288]{1,0:T(8,128)(2,1)} async-done(((bf16[128,384]{1,0:T(8,128)(2,1)}), bf16[128,12288]{1,0:T(8,128)(2,1)}) %all-gather.10.cloned.1.call-update) | async-done | bytes 3145744 | tf_op jit(solution)/shard_map/all_gather | solution.py:112
  196.1 2.5 gather_fusion.1
  198.9 2.7 fusion.8
  202.9 2.3 reshape.289
  205.2 1.9 copy.131
  207.1 2.3 reshape.290
  209.4 1.9 copy.129
  211.3 2.3 reshape.291
  213.6 1.9 copy.130
  215.5 5.6 fusion.79
  221.1 3.0 fusion.19
  225.9 2.9 reshape.262
  229.9 2.0 convolution_add_fusion.7
  236.0 80.9 %all-gather.16.cloned.1.call-done = bf16[768,3072]{1,0:T(8,128)(2,1)} async-done(((bf16[768,768]{1,0:T(8,128)(2,1)}), bf16[768,3072]{1,0:T(8,128)(2,1)}) %all-gather.16.cloned.1.call-update) | async-done | bytes 4718608 | tf_op jit(solution)/shard_map/all_gather | solution.py:101
  316.9 4.4 fusion.82
  321.3 4.6 multiply_convert_fusion.1
  325.8 80.5 %all-gather.20.cloned.1.call-done = bf16[3072,768]{0,1:T(8,128)(2,1)} async-done(((bf16[768,768]{0,1:T(8,128)(2,1)}), bf16[3072,768]{0,1:T(8,128)(2,1)}) %all-gather.20.cloned.1.call-update) | async-done | bytes 4718608 | tf_op jit(solution)/shard_map/all_gather | solution.py:101
  406.3 4.7 fusion.83
  411.1 2.6 fusion.6
  415.1 2.1 fusion.84
  422.0 3.1 reshape.292
  425.1 3.1 copy.141
  428.2 4.1 multiply_reduce_fusion
  432.3 3.6 multiply_convert_fusion
  444.3 3.2 reshape.266
  447.5 2.2 constant_dynamic-update-slice_fusion.2
  451.4 3.2 reshape.267
  454.6 2.8 copy.151
  457.4 3.4 reshape.268
  460.8 2.2 constant_dynamic-update-slice_fusion.1
  463.9 2.3 fusion.38
  471.1 3.7 fusion.48
  474.8 4.8 convolution_add_fusion.8
  479.6 2.0 fusion.18
  484.2 3.5 all-to-all-start.1
  487.8 3.8 fusion.85
  496.9 3.5 all-to-all-start.3
  501.6 7.1 %all-to-all-done.3 = bf16[2,196,768]{2,0,1:T(2,128)(2,1)S(1)} async-done(((bf16[2,196,768]{2,0,1:T(2,128)(2,1)}), bf16[2,196,768]{2,0,1:T(2,128)(2,1)S(1)}, u32[]{:S(2)}, u32[]{:S(2)}) %all-to-all-start.3) | async-done | bytes 602144 | tf_op jit(solution)/shard_map/all_to_all | solution.py:88
  509.9 77.8 %reduce-scatter.2.cloned.1.call-done = f32[128,384]{1,0:T(8,128)} async-done(((f32[128,12288]{1,0:T(8,128)}), f32[128,384]{1,0:T(8,128)}) %reduce-scatter.2.cloned.1.call-update) | async-done | bytes 196624 | tf_op jit(solution)/shard_map/reduce_scatter | solution.py:208
  (189 shorter events, 56.6 us)
Async XLA Ops:
  7.2 37.3 %copy-start = (s32[4]{0:T(128)S(1)}, s32[4]{0:T(128)}, u32[]{:S(2)}) copy-start(s32[4]{0:T(128)} %param.14) | copy-start | bytes 52
  7.2 32.2 %all-gather.14.cloned.1.call-start = ((), (), s32[]{:S(2)}) async-start(), calls=%async_computation.8 | async-start | bytes 1327104 | tf_op jit(solution)/shard_map/all_gather | solution.py:102
  7.9 56.9 %all-gather.18.cloned.1.call-start = ((), (), s32[]{:S(2)}) async-start(), calls=%async_computation.10 | async-start | bytes 1327104 | tf_op jit(solution)/shard_map/all_gather | solution.py:102
  8.7 127.7 %all-gather.8.cloned.1.call-start = ((), (), s32[]{:S(2)}) async-start(), calls=%async_computation.5 | async-start | bytes 4423680 | tf_op jit(solution)/shard_map/all_gather | solution.py:101
  25.9 2.2 copy-start.30
  25.9 3.0 copy-start.36
  28.0 11.9 %copy-start.32 = (bf16[4,98,768]{2,0,1:T(4,128)(2,1)S(1)}, bf16[4,98,768]{2,0,1:T(4,128)(2,1)}, u32[]{:S(2)}) copy-start(bf16[4,98,768]{2,0,1:T(4,128)(2,1)} %param.12) | copy-start | bytes 1806340
  28.0 168.1 %all-gather.10.cloned.1.call-start = ((), (), s32[]{:S(2)}) async-start(), calls=%async_computation.6 | async-start | bytes 3244032 | tf_op jit(solution)/shard_map/all_gather | solution.py:112
  28.8 201.1 %all-gather.12.cloned.1.call-start = ((), (), s32[]{:S(2)}) async-start(), calls=%async_computation.7 | async-start | bytes 1474560 | tf_op jit(solution)/shard_map/all_gather | solution.py:101
  39.3 277.6 %all-gather.16.cloned.1.call-start = ((), (), s32[]{:S(2)}) async-start(), calls=%async_computation.9 | async-start | bytes 5898240 | tf_op jit(solution)/shard_map/all_gather | solution.py:101
  39.9 5.3 copy-start.33
  40.8 13.5 %all-to-all-start = ((bf16[4,98,768]{2,1,0:T(8,128)(2,1)}), bf16[4,98,768]{2,1,0:T(8,128)(2,1)S(1)}, u32[]{:S(2)}, u32[]{:S(2)}) async-start(bf16[4,98,768]{2,1,0:T(8,128)(2,1)} %copy.122), calls=%async_computation | async-start | bytes 1277952 | tf_op jit(solution)/shard_map/all_to_all | solution.py:83
  54.3 14.3 %all-to-all-start.2 = ((bf16[4,98,768]{2,1,0:T(8,128)(2,1)}), bf16[4,98,768]{2,1,0:T(8,128)(2,1)}, u32[]{:S(2)}, u32[]{:S(2)}) async-start(bf16[4,98,768]{2,1,0:T(8,128)(2,1)} %copy.138), calls=%async_computation.2 | async-start | bytes 1277952 | tf_op jit(solution)/shard_map/all_to_all | solution.py:83
  58.6 347.7 %all-gather.20.cloned.1.call-start = ((), (), s32[]{:S(2)}) async-start(), calls=%async_computation.11 | async-start | bytes 5898240 | tf_op jit(solution)/shard_map/all_gather | solution.py:101
  64.8 522.9 %reduce-scatter.2.cloned.1.call-start = ((), (), s32[]{:S(2)}) async-start(), calls=%async_computation.12 | async-start | bytes 6488064 | tf_op jit(solution)/shard_map/reduce_scatter | solution.py:208
  66.6 163.3 %copy-start.2 = (f32[392,768]{1,0:T(8,128)}, f32[392,768]{1,0:T(8,128)S(1)}, u32[]{:S(2)}) copy-start(f32[392,768]{1,0:T(8,128)S(1)} %reshape.270) | copy-start | bytes 3612676
  69.9 165.0 %copy-start.13 = (bf16[392,768]{1,0:T(8,128)(2,1)}, bf16[392,768]{1,0:T(8,128)(2,1)S(1)}, u32[]{:S(2)}) copy-start(bf16[392,768]{1,0:T(8,128)(2,1)S(1)} %reshape.264) | copy-start | bytes 1806340
  70.1 128.5 %copy-start.24 = (bf16[392,768]{1,0:T(8,128)(2,1)}, bf16[392,768]{1,0:T(8,128)(2,1)S(1)}, u32[]{:S(2)}) copy-start(bf16[392,768]{1,0:T(8,128)(2,1)S(1)} %multiply_convert_fusion.6) | copy-start | bytes 1806340
  198.6 3.0 copy-start.16
  215.5 5.6 copy-start.28
  231.9 1.6 copy-start.38
  233.1 1.7 copy-start.7
  233.7 83.2 %copy-start.26 = (bf16[392,768]{1,0:T(8,128)(2,1)}, bf16[392,768]{1,0:T(8,128)(2,1)S(1)}, u32[]{:S(2)}) copy-start(bf16[392,768]{1,0:T(8,128)(2,1)S(1)} %multiply_convert_fusion.5) | copy-start | bytes 1806340
  406.3 4.7 copy-start.17
  406.3 4.7 copy-start.18
  406.3 8.8 %slice-start.2 = ((s8[4718592]{0:T(1024)(128)(4,1)}), s8[4194304]{0:T(1024)(128)(4,1)S(1)}, s32[]{:S(2)}) async-start(s8[4718592]{0:T(1024)(128)(4,1)} %bitcast.140), calls=%async_computation.15 | async-start | bytes 8388608
  411.1 4.1 slice-start.3
  415.1 2.1 copy-start.8
  418.8 1.7 copy-start.19
  428.2 10.7 %slice-start = ((s8[4915200]{0:T(1024)(128)(4,1)}), s8[4194304]{0:T(1024)(128)(4,1)S(1)}, s32[]{:S(2)}) async-start(s8[4915200]{0:T(1024)(128)(4,1)} %bitcast.132), calls=%async_computation.13 | async-start | bytes 8388608
  432.3 3.7 copy-start.23
  432.3 6.6 %slice-start.1 = ((s8[4915200]{0:T(1024)(128)(4,1)}), s8[720896]{0:T(1024)(128)(4,1)S(1)}, s32[]{:S(2)}) async-start(s8[4915200]{0:T(1024)(128)(4,1)} %bitcast.132), calls=%async_computation.14 | async-start | bytes 1441792
  437.1 1.8 copy-start.29
  447.5 2.2 copy-start.21
  460.8 2.2 copy-start.20
  463.9 2.3 copy-start.25
  463.9 2.6 copy-start.11
  466.6 1.5 copy-start.27
  467.3 1.8 copy-start.10
  481.6 6.2 %copy-start.12 = (bf16[392,2304]{0,1:T(8,128)(2,1)S(1)}, bf16[392,2304]{0,1:T(8,128)(2,1)}, u32[]{:S(2)}) copy-start(bf16[392,2304]{0,1:T(8,128)(2,1)} %constant_dynamic-update-slice_fusion) | copy-start | bytes 5419012
  484.2 12.7 %all-to-all-start.1 = ((bf16[2,196,768]{2,0,1:T(2,128)(2,1)}), bf16[2,196,768]{2,0,1:T(2,128)(2,1)S(1)}, u32[]{:S(2)}, u32[]{:S(2)}) async-start(bf16[2,196,768]{2,0,1:T(2,128)(2,1)} %copy.136), calls=%async_computation.1 | async-start | bytes 1204224 | tf_op jit(solution)/shard_map/all_to_all | solution.py:88
  487.8 3.8 copy-start.3
  491.6 1.6 copy-start.6
  496.9 11.8 %all-to-all-start.3 = ((bf16[2,196,768]{2,0,1:T(2,128)(2,1)}), bf16[2,196,768]{2,0,1:T(2,128)(2,1)S(1)}, u32[]{:S(2)}, u32[]{:S(2)}) async-start(bf16[2,196,768]{2,0,1:T(2,128)(2,1)} %copy.152), calls=%async_computation.3 | async-start | bytes 1204224 | tf_op jit(solution)/shard_map/all_to_all | solution.py:88
  500.5 87.2 %copy-start.31 = (f32[128,384]{1,0:T(8,128)S(1)}, f32[128,384]{1,0:T(8,128)}, u32[]{:S(2)}) copy-start(f32[128,384]{1,0:T(8,128)} %param.21) | copy-start | bytes 589828
  500.5 87.2 %copy-start.34 = (f32[128,384]{1,0:T(8,128)S(1)}, f32[128,384]{1,0:T(8,128)}, u32[]{:S(2)}) copy-start(f32[128,384]{1,0:T(8,128)} %param.22) | copy-start | bytes 589828
  500.5 87.2 %copy-start.35 = (f32[128,384]{1,0:T(8,128)S(1)}, f32[128,384]{1,0:T(8,128)}, u32[]{:S(2)}) copy-start(f32[128,384]{1,0:T(8,128)} %param.23) | copy-start | bytes 589828
  508.7 80.8 %copy-start.1 = (s32[4]{0:T(128)S(1)}, s32[4]{0:T(128)}, u32[]{:S(2)}) copy-start(s32[4]{0:T(128)} %param.14) | copy-start | bytes 52
  (7 other events, 7.7 us)
Sparse Core Ops, SparseCore 0:
  9.9 28.9 all-gather.13
  40.8 23.9 all-gather.17
  66.4 69.9 all-gather.7
  139.7 56.3 all-gather.9
  197.5 29.3 all-gather.11
  228.3 88.5 all-gather.15
  318.5 87.8 all-gather.19
  474.9 112.7 reduce-scatter.1

commit v2 on v1

--- a/solution.py
+++ b/solution.py
@@ -3,6 +3,8 @@
 import jax
 import jax.numpy as jnp
 from jax import lax
+from jax.experimental import pallas as pl
+from jax.experimental.pallas import tpu as pltpu
 from jax.sharding import PartitionSpec as P
 
 HEAD = 64
@@ -47,6 +49,23 @@
     first = jnp.mean(scaled, axis=-1, keepdims=True)
     second = jnp.mean(scaled * unit, axis=-1, keepdims=True)
     return inverse * (scaled - first - unit * second)
+
+
+def adam(owner_grad, adapters, moment_one, moment_two):
+    first_moment = beta_first * moment_one + (1.0 - beta_first) * owner_grad
+    second_moment = beta_second * moment_two + (1.0 - beta_second) * owner_grad * owner_grad
+    first_hat = first_moment / (1.0 - beta_first**STEP)
+    second_hat = second_moment / (1.0 - beta_second**STEP)
+    updated = adapters - learn_rate * (
+        first_hat / (jnp.sqrt(second_hat) + adam_epsilon) + weight_decay * adapters
+    )
+    return (
+        owner_grad,
+        updated,
+        first_moment,
+        second_moment,
+        updated.astype(jnp.bfloat16),
+    )
 
 
 def shards(
@@ -208,29 +227,691 @@
     owner_grad = lax.psum_scatter(
         dot(pick, grads), ("dp", "mp"), scatter_dimension=1, tiled=True
     )
-    first_moment = beta_first * moment_one + (1.0 - beta_first) * owner_grad
-    second_moment = beta_second * moment_two + (1.0 - beta_second) * owner_grad * owner_grad
-    first_hat = first_moment / (1.0 - beta_first**STEP)
-    second_hat = second_moment / (1.0 - beta_second**STEP)
-    updated = adapters - learn_rate * (
-        first_hat / (jnp.sqrt(second_hat) + adam_epsilon) + weight_decay * adapters
-    )
-    return (
-        swap_back(outputs),
-        swap_back(input_grad),
-        owner_grad,
-        updated,
-        first_moment,
-        second_moment,
-        updated.astype(jnp.bfloat16),
-    )
+    return (swap_back(outputs), swap_back(input_grad)) + adam(
+        owner_grad, adapters, moment_one, moment_two
+    )
+
+
+MESH = pl.DeviceIdType.MESH
+X1, Y1, Y2, X2, C0, C1A, C1B, C2A, C2B = range(9)
+HALF_PITCH = 104
+HALF_SLOT = 112
+
+
+def fused_kernel(
+    tok_ref,
+    cot_ref,
+    g1_ref,
+    g2_ref,
+    shard_ref,
+    adp_ref,
+    act_ref,
+    ing_ref,
+    gr_ref,
+    wa,
+    wf,
+    ad,
+    ts,
+    cs,
+    tr,
+    cr,
+    xf,
+    dyb,
+    n1,
+    n2,
+    proj,
+    soft,
+    att,
+    mid,
+    acc,
+    dn,
+    tmp,
+    buf,
+    dbr,
+    dpj,
+    bq,
+    ao,
+    bu,
+    an,
+    gq,
+    go,
+    g16,
+    gc,
+    gs,
+    rb,
+    osend,
+    isend,
+    smalls,
+    zs,
+    zr,
+    azs,
+    azr,
+    ss,
+    rs,
+    ps,
+    pr,
+    cxs,
+    cxr,
+    us,
+    ur,
+):
+    dp = lax.axis_index("dp")
+    z = lax.axis_index("mp")
+    y = dp // 4
+    x = lax.rem(dp // 2, 2)
+    c = lax.rem(dp, 2)
+    h = lax.rem(z, 2)
+    zp = z + 1 - 2 * h
+    zn = 4
+    shard_rows = tok_ref.shape[1]
+    rows = xf.shape[0]
+    frame_rows = rows // 2
+    width = xf.shape[1]
+    local = width // zn
+    scale = 1.0 / math.sqrt(HEAD)
+
+    def place(yy, xx, cc, zz):
+        return ((yy * 2 + xx) * 2 + cc, zz)
+
+    barrier = pltpu.get_barrier_semaphore()
+    for k in range(1, 16):
+        yx = lax.rem(y * 2 + x + k // 4, 4)
+        target = (yx * 2 + c, lax.rem(z + k % 4, 4))
+        pl.semaphore_signal(barrier, inc=1, device_id=target, device_id_type=MESH)
+    pl.semaphore_signal(barrier, inc=1, device_id=place(y, x, 1 - c, z), device_id_type=MESH)
+
+    def remote(src, dst, send, recv, target):
+        return pltpu.make_async_remote_copy(
+            src_ref=src,
+            dst_ref=dst,
+            send_sem=send,
+            recv_sem=recv,
+            device_id=target,
+            device_id_type=MESH,
+        )
+
+    wa[z, y, x, c] = shard_ref[0]
+    wf[z, 0, y, x, c] = shard_ref[1]
+    wf[z, 1, y, x, c] = shard_ref[2]
+    for m in range(4):
+        ts[m, pl.ds(96, 16)] = jnp.zeros((16, width), jnp.bfloat16)
+        cs[m, pl.ds(96, 16)] = jnp.zeros((16, width), jnp.bfloat16)
+        ts[m, pl.ds(0, shard_rows)] = tok_ref[m]
+        cs[m, pl.ds(0, shard_rows)] = cot_ref[m]
+    span = adp_ref.shape[2]
+    low_columns = pl.ds(pl.multiple_of(lax.rem(z, 2) * span, 128), span)
+    ad[y, x, c, z // 2, :, low_columns] = adp_ref[h]
+
+    def part(s, zk, yy, xx, cc, first, count):
+        if s == 0:
+            return wa.at[zk, yy, xx, cc, pl.ds(first, count), :]
+        if s == 1:
+            return wf.at[zk, :, yy, xx, cc, pl.ds(first, count), :]
+        return ad.at[yy, xx, cc, :, pl.ds(first, count), :]
+
+    def move(s, k, what):
+        full = 32 if s == 2 else 96
+        n = full // 2
+        zk = lax.rem(z + k, zn)
+        every = pl.ds(0, 2)
+        args, target = {
+            X1: ((y, x, c, 0, n), (y, 1 - x, c)),
+            Y1: ((y, x, c, n, n), (1 - y, x, c)),
+            Y2: ((y, every, c, 0, n), (1 - y, x, c)),
+            X2: ((every, x, c, n, n), (y, 1 - x, c)),
+            C0: ((y, x, c, 0, full), (y, x, 1 - c)),
+            C1A: ((y, 1 - x, c, 0, n), (y, x, 1 - c)),
+            C1B: ((1 - y, x, c, n, n), (y, x, 1 - c)),
+            C2A: ((1 - y, every, c, 0, n), (y, x, 1 - c)),
+            C2B: ((every, 1 - x, c, n, n), (y, x, 1 - c)),
+        }[what]
+        ref = part(s, zk, *args)
+        index = s * 4 + k
+        return remote(ref, ref, ss.at[index, what], rs.at[index, what], place(*target, z))
+
+    def z_move(s, j):
+        ref = part(s, z, y, x, c, 0, 96)
+        return remote(ref, ref, zs.at[s, j], zr.at[s, j], (dp, lax.rem(z + zn - j, zn)))
+
+    def ad_move(j):
+        other = lax.rem(z + zn - j, zn)
+        dst = ad.at[y, x, c, z // 2, :, low_columns]
+        return remote(adp_ref.at[lax.rem(other, 2)], dst, azs.at[j], azr.at[j], (dp, other))
+
+    def t1(s, k):
+        if s < 2:
+            if isinstance(k, int):
+                if k:
+                    z_move(s, k).wait_recv()
+            else:
+
+                @pl.when(k > 0)
+                def _():
+                    z_move(s, k).wait_recv()
+
+        for what in (X1, Y1, C0):
+            move(s, k, what).start()
+
+    def t2(s, k):
+        move(s, k, X1).wait_recv()
+        move(s, k, Y2).start()
+        move(s, k, Y1).wait_recv()
+        move(s, k, X2).start()
+        move(s, k, C1A).start()
+        move(s, k, C1B).start()
+
+    def t3(s, k):
+        move(s, k, Y2).wait_recv()
+        move(s, k, C2A).start()
+        move(s, k, X2).wait_recv()
+        move(s, k, C2B).start()
+
+    def ready(s, k):
+        for what in (C0, C1A, C1B, C2A, C2B):
+            move(s, k, what).wait_recv()
+
+    tok_move = remote(
+        ts.at[pl.ds(2 - 2 * h, 2)], tr, ps.at[0], pr.at[0], (dp, zp)
+    )
+    cot_move = remote(
+        cs.at[pl.ds(2 - 2 * h, 2)], cr, ps.at[1], pr.at[1], (dp, zp)
+    )
+    act_move = remote(
+        osend, act_ref.at[pl.ds(2 * h, 2)], ps.at[2], pr.at[2], (dp, zp)
+    )
+    ing_move = remote(
+        isend, ing_ref.at[pl.ds(2 * h, 2)], ps.at[3], pr.at[3], (dp, zp)
+    )
+
+    pl.semaphore_wait(barrier, 16)
+    for j in range(1, 4):
+        ad_move(j).start()
+    tok_move.start()
+    t1(0, 0)
+    for j in range(1, 4):
+        z_move(0, j).start()
+    cot_move.start()
+    for j in range(1, 4):
+        z_move(1, j).start()
+    for j in range(1, 4):
+        ad_move(j).wait_recv()
+    t1(2, 0)
+    t1(0, 1)
+    t2(0, 0)
+    t2(2, 0)
+
+    def dot(left, right):
+        return jnp.dot(left, right, preferred_element_type=jnp.float32)
+
+    def dot_t(left, right):
+        return lax.dot_general(
+            left, right, (((1,), (1,)), ((), ())), preferred_element_type=jnp.float32
+        )
+
+    def t_dot(left, right):
+        return lax.dot_general(
+            left, right, (((0,), (0,)), ((), ())), preferred_element_type=jnp.float32
+        )
+
+    row_frame = lax.broadcasted_iota(jnp.int32, (rows, 32), 0) // frame_rows
+    column_frame = lax.broadcasted_iota(jnp.int32, (rows, 32), 1) // RANK
+    mask = row_frame == column_frame
+
+    def low(values):
+        return jnp.where(mask, values, 0.0).astype(jnp.bfloat16)
+
+    def tiles(body, step=16):
+        @pl.loop(0, rows // step)
+        def _(t):
+            body(pl.ds(pl.multiple_of(t * step, step), step))
+
+    def norm_parts(values):
+        center = values - jnp.mean(values, axis=-1, keepdims=True)
+        spread = jnp.mean(center * center, axis=-1, keepdims=True)
+        inverse = lax.rsqrt(spread + norm_epsilon)
+        return center * inverse, inverse
+
+    def norm_back(values, gain, grad):
+        unit, inverse = norm_parts(values)
+        scaled = grad * gain
+        first = jnp.mean(scaled, axis=-1, keepdims=True)
+        second = jnp.mean(scaled * unit, axis=-1, keepdims=True)
+        return inverse * (scaled - first - unit * second)
+
+    def group(g):
+        return ad[g // 8, (g // 4) % 2, (g // 2) % 2, g % 2]
+
+    def group_ref(g):
+        return g16.at[g // 8, (g // 4) % 2, (g // 2) % 2, g % 2]
+
+    def attn_block(zk):
+        return wa[zk].reshape(width, width)
+
+    def halves(f):
+        own = pl.ds(pl.multiple_of(f * frame_rows + h * HALF_PITCH, 8), HALF_PITCH)
+        other = pl.ds(pl.multiple_of(f * frame_rows + (1 - h) * HALF_PITCH, 8), HALF_PITCH)
+        return own, other
+
+    def join(dst, own_slots, other_slots):
+        for f in range(2):
+            own, other = halves(f)
+            dst[own] = own_slots[2 * h + f][:HALF_PITCH].astype(jnp.float32)
+            dst[other] = other_slots[f][:HALF_PITCH].astype(jnp.float32)
+
+    tok_move.wait_recv()
+    join(xf, ts, tr)
+
+    def first_norm(at):
+        values = xf[at]
+        unit, _ = norm_parts(values)
+        n1[at] = (unit * g1_ref[...]).astype(jnp.bfloat16)
+        mid[at] = values
+
+    tiles(first_norm)
+    t3(2, 0)
+    ready(2, 0)
+    for k in range(4):
+        bq[k] = jnp.concatenate(
+            [jnp.zeros((32, local), jnp.bfloat16)]
+            + [group(1 + i)[:, k * local : (k + 1) * local] for i in range(3)],
+            axis=1,
+        )
+        ao[k] = group(4)[:, k * local : (k + 1) * local]
+        bu[k] = group(7 + k)
+        an[k] = group(11 + k)
+    smalls[0] = low(dot_t(n1[...], group(0)))
+    key_pad = (
+        lax.rem(lax.broadcasted_iota(jnp.int32, (frame_rows, 1), 0), HALF_PITCH) >= shard_rows
+    )
+    bias = jnp.where(key_pad, -1e30, 0.0).astype(jnp.float32)
+
+    LOW_QKV, LOW_OUT, LOW_UP, LOW_DOWN, THR_DOWN, THR_UP, THR_OUT, THR_QKV = range(8)
+
+    def attention(i, out_low):
+        zk = lax.rem(z + i, zn)
+        block = attn_block(zk)
+        proj[zk] = (dot(n1[...], block) + dot(smalls[LOW_QKV], bq[zk])).astype(jnp.bfloat16)
+        for f in range(2):
+            at = pl.ds(f * frame_rows, frame_rows)
+            for head in range(3):
+                first = local + head * HEAD
+                q = proj[zk, at, first : first + HEAD]
+                k = proj[zk, at, first + local : first + local + HEAD]
+                v = proj[zk, at, first + 2 * local : first + 2 * local + HEAD]
+                scores = dot_t(k, q) * scale + bias
+                exponent = jnp.exp(scores - jnp.max(scores, axis=0, keepdims=True))
+                weights = exponent / jnp.sum(exponent, axis=0, keepdims=True)
+                weights = weights.astype(jnp.bfloat16)
+                soft[zk, f * 3 + head] = weights
+                att[zk, at, head * HEAD : (head + 1) * HEAD] = (
+                    t_dot(weights, v).astype(jnp.bfloat16)
+                )
+        gathered = att[zk]
+        mid[...] += dot_t(gathered, block[:, :local])
+        return out_low + dot_t(gathered, ao[zk])
+
+    def attention_step(i, out_low):
+        @pl.when(i < 2)
+        def _():
+            t1(0, i + 2)
+
+        @pl.when(i >= 2)
+        def _():
+            t1(1, i - 2)
+
+        @pl.when(i < 3)
+        def _():
+            t2(0, i + 1)
+
+        @pl.when(i == 3)
+        def _():
+            t2(1, 0)
+
+        t3(0, i)
+        ready(0, i)
+        return attention(i, out_low)
+
+    out_low = lax.fori_loop(0, 4, attention_step, jnp.zeros((rows, 32), jnp.float32))
+    smalls[LOW_OUT] = low(out_low)
+    mid[...] += dot(smalls[LOW_OUT], group(5))
+
+    def second_norm(at):
+        unit, _ = norm_parts(mid[at])
+        n2[at] = (unit * g2_ref[...]).astype(jnp.bfloat16)
+
+    tiles(second_norm)
+    cot_move.wait_recv()
+    join(tmp, cs, cr)
+    dyb[...] = tmp[...].astype(jnp.bfloat16)
+    smalls[LOW_UP] = low(dot_t(n2[...], group(6)))
+    smalls[THR_DOWN] = low(dot_t(dyb[...], group(15)))
+    group_ref(15)[...] = jnp.zeros((32, width), jnp.bfloat16)
+    acc[...] = mid[...]
+    dn[...] = jnp.zeros_like(dn)
+
+    def feed(i, lows):
+        down_low, up_back = lows
+        zk = lax.rem(z + i, zn)
+        up = wf[zk, 0].reshape(width, width)
+        down = wf[zk, 1].reshape(width, width)
+        tmp[...] = dot(n2[...], up) + dot(smalls[LOW_UP], bu[zk])
+
+        def gate(at):
+            hidden = tmp[at]
+            phi = 0.5 + 0.5 * lax.erf(hidden * math.sqrt(0.5))
+            bell = jnp.exp(-0.5 * hidden * hidden) * (1.0 / math.sqrt(2.0 * math.pi))
+            buf[0, at] = (hidden * phi).astype(jnp.bfloat16)
+            tmp[at] = phi + hidden * bell
+
+        tiles(gate)
+        active = buf[0]
+        acc[...] += dot_t(active, down)
+        tmp[...] = tmp[...] * (dot(dyb[...], down) + dot(smalls[THR_DOWN], an[zk]))
+        buf[1] = tmp[...].astype(jnp.bfloat16)
+        d_hidden = buf[1]
+        dn[...] += dot_t(d_hidden, up)
+        gu = 7 + zk
+        ga = 11 + zk
+        g16[gu // 8, lax.rem(gu // 4, 2), lax.rem(gu // 2, 2), lax.rem(gu, 2)] = t_dot(
+            smalls[LOW_UP], d_hidden
+        ).astype(jnp.bfloat16)
+        g16[ga // 8, lax.rem(ga // 4, 2), lax.rem(ga // 2, 2), lax.rem(ga, 2)] = t_dot(
+            smalls[THR_DOWN], active
+        ).astype(jnp.bfloat16)
+        return down_low + dot_t(active, an[zk]), up_back + dot_t(d_hidden, bu[zk])
+
+    def feed_step(i, lows):
+        @pl.when(i < 2)
+        def _():
+            t1(1, i + 2)
+
+        @pl.when(i < 3)
+        def _():
+            t2(1, i + 1)
+
+        t3(1, i)
+        ready(1, i)
+        return feed(i, lows)
+
+    empty = jnp.zeros((rows, 32), jnp.float32)
+    down_low, up_back = lax.fori_loop(0, 4, feed_step, (empty, empty))
+    smalls[LOW_DOWN] = low(down_low)
+    smalls[THR_UP] = low(up_back)
+    group_ref(15)[...] = t_dot(smalls[LOW_DOWN], dyb[...]).astype(jnp.bfloat16)
+
+    def core_move(yx):
+        src = g16.at[yx // 2, yx % 2, 1 - c]
+        return remote(src, gc.at[yx], cxs.at[yx], cxr.at[yx], place(y, x, 1 - c, z))
+
+    def owner_move(yx, zz):
+        back_yx = lax.rem(y * 2 + x + 4 - yx, 4)
+        back_z = lax.rem(z + 4 - zz, 4)
+        slot = back_yx * 4 + back_z
+        src = gs.at[yx, zz // 2, :, pl.ds((zz % 2) * span, span)]
+        copy = remote(src, rb.at[slot], us.at[yx, zz], ur.at[slot], (yx * 2 + c, zz))
+        return copy, slot
+
+    def spread_out(yx):
+        core_move(yx).wait_recv()
+        for g in range(2):
+            gs[yx, g] = (
+                g16[yx // 2, yx % 2, c, g].astype(jnp.float32) + gc[yx, g].astype(jnp.float32)
+            ).astype(jnp.bfloat16)
+        for zz in range(4):
+            copy, slot = owner_move(yx, zz)
+
+            @pl.when(slot != 0)
+            def _():
+                copy.start()
+
+            @pl.when(slot == 0)
+            def _():
+                rb[0] = gs[yx, zz // 2, :, pl.ds((zz % 2) * span, span)]
+
+    core_move(3).start()
+    core_move(2).start()
+
+    dn[...] += dot(smalls[THR_UP], group(6))
+    group_ref(6)[...] = t_dot(smalls[THR_UP], n2[...]).astype(jnp.bfloat16)
+    acc[...] += dot(smalls[LOW_DOWN], group(15))
+
+    def second_back(at):
+        value = dyb[at].astype(jnp.float32) + norm_back(mid[at], g2_ref[...], dn[at])
+        dn[at] = value
+        dbr[at] = value.astype(jnp.bfloat16)
+
+    tiles(second_back)
+    for f in range(2):
+        own, other = halves(f)
+        osend[f, pl.ds(0, HALF_PITCH)] = acc[other].astype(jnp.bfloat16)
+        act_ref[2 * h + f, pl.ds(0, HALF_PITCH)] = acc[own].astype(jnp.bfloat16)
+    act_move.start()
+    smalls[THR_OUT] = low(dot_t(dbr[...], group(5)))
+    group_ref(5)[...] = t_dot(smalls[LOW_OUT], dbr[...]).astype(jnp.bfloat16)
+    dpj[:, 0:local] = jnp.zeros((rows, local), jnp.bfloat16)
+    acc[...] = jnp.zeros_like(acc)
+
+    spread_out(3)
+    spread_out(2)
+
+    def attention_back(zk, qkv_back):
+        block = attn_block(zk)
+        d_att = (dot(dbr[...], block[:, :local]) + dot(smalls[THR_OUT], ao[zk])).astype(
+            jnp.bfloat16
+        )
+        buf[0, :, 0:local] = d_att
+        go[zk] = t_dot(smalls[THR_OUT], att[zk]).astype(jnp.bfloat16)
+        for f in range(2):
+            at = pl.ds(f * frame_rows, frame_rows)
+            for head in range(3):
+                first = local + head * HEAD
+                q = proj[zk, at, first : first + HEAD]
+                k = proj[zk, at, first + local : first + local + HEAD]
+                v = proj[zk, at, first + 2 * local : first + 2 * local + HEAD]
+                d_out = buf[0, at, head * HEAD : (head + 1) * HEAD]
+                weights = soft[zk, f * 3 + head]
+                d_values = dot(weights, d_out)
+                d_soft = dot_t(v, d_out)
+                wide = weights.astype(jnp.float32)
+                inner = jnp.sum(wide * d_soft, axis=0, keepdims=True)
+                d_scores = (wide * (d_soft - inner)).astype(jnp.bfloat16)
+                d_keys = dot(d_scores, q) * scale
+                d_queries = t_dot(d_scores, k) * scale
+                dpj[at, first : first + HEAD] = d_queries.astype(jnp.bfloat16)
+                dpj[at, first + local : first + local + HEAD] = d_keys.astype(jnp.bfloat16)
+                dpj[at, first + 2 * local : first + 2 * local + HEAD] = d_values.astype(
+                    jnp.bfloat16
+                )
+        d_projected = dpj[...]
+        gq[zk] = t_dot(smalls[LOW_QKV], d_projected).astype(jnp.bfloat16)
+        acc[...] += dot_t(d_projected, block)
+        return qkv_back + dot_t(d_projected, bq[zk])
+
+    qkv_back = lax.fori_loop(0, 4, attention_back, empty)
+    smalls[THR_QKV] = low(qkv_back)
+    group_ref(0)[...] = t_dot(smalls[THR_QKV], n1[...]).astype(jnp.bfloat16)
+    for i in range(3):
+        first = (1 + i) * local
+        group_ref(1 + i)[...] = jnp.concatenate(
+            [gq[k][:, first : first + local] for k in range(4)], axis=1
+        )
+    group_ref(4)[...] = jnp.concatenate([go[k] for k in range(4)], axis=1)
+    core_move(1).start()
+    core_move(0).start()
+
+    acc[...] += dot(smalls[THR_QKV], group(0))
+
+    def first_back(at):
+        acc[at] = dn[at] + norm_back(xf[at], g1_ref[...], acc[at])
+
+    tiles(first_back)
+    for f in range(2):
+        own, other = halves(f)
+        isend[f, pl.ds(0, HALF_PITCH)] = acc[other].astype(jnp.bfloat16)
+        ing_ref[2 * h + f, pl.ds(0, HALF_PITCH)] = acc[own].astype(jnp.bfloat16)
+    ing_move.start()
+    spread_out(1)
+    spread_out(0)
+
+    for slot in range(1, 16):
+        remote(rb.at[slot], rb.at[slot], us.at[0, 0], ur.at[slot], (dp, zp)).wait_recv()
+    for parity in range(2):
+        total = jnp.zeros((32, span), jnp.float32)
+        for slot in range(16):
+            if slot % 2 == parity:
+                total = total + rb[slot].astype(jnp.float32)
+        gr_ref[lax.rem(h + parity, 2)] = total
+    for yx in range(4):
+        core_move(yx).wait_send()
+        for zz in range(4):
+            copy, slot = owner_move(yx, zz)
+
+            @pl.when(slot != 0)
+            def _():
+                copy.wait_send()
+
+    tok_move.wait_send()
+    cot_move.wait_send()
+    for j in range(1, 4):
+        ad_move(j).wait_send()
+        z_move(0, j).wait_send()
+        z_move(1, j).wait_send()
+
+    @pl.loop(0, 4)
+    def _(k):
+        for what in range(9):
+            move(0, k, what).wait_send()
+            move(1, k, what).wait_send()
+
+    for what in range(9):
+        move(2, 0, what).wait_send()
+    act_move.wait()
+    ing_move.wait()
+
+
+def fused(
+    tokens,
+    cotangent,
+    clip_adapter,
+    gain_one,
+    gain_two,
+    w_qkv,
+    w_out,
+    w_up,
+    w_down,
+    adapters,
+    moment_one,
+    moment_two,
+):
+    micro_count, shard_rows, width = tokens.shape
+    rank_all, span = adapters.shape
+    shard = jnp.stack(
+        [
+            jnp.concatenate([w_out.T, w_qkv.reshape(w_qkv.shape[0], -1)], axis=1),
+            w_up,
+            w_down.T,
+        ]
+    )
+    picked = adapters.astype(jnp.bfloat16).reshape(rank_all // RANK, RANK, span)[clip_adapter]
+    adp = picked.reshape(2, 2 * RANK, span)
+    rows = 4 * HALF_PITCH
+    frame_rows = 2 * HALF_PITCH
+    local = width // 4
+    bf, f32 = jnp.bfloat16, jnp.float32
+    vmem = pl.BlockSpec(memory_space=pltpu.VMEM)
+    scratch = [
+        pltpu.VMEM((4, 2, 2, 2, 96, width), bf),
+        pltpu.VMEM((4, 2, 2, 2, 2, 96, width), bf),
+        pltpu.VMEM((2, 2, 2, 2, 32, width), bf),
+        pltpu.VMEM((4, HALF_SLOT, width), bf),
+        pltpu.VMEM((4, HALF_SLOT, width), bf),
+        pltpu.VMEM((2, HALF_SLOT, width), bf),
+        pltpu.VMEM((2, HALF_SLOT, width), bf),
+        pltpu.VMEM((rows, width), f32),
+        pltpu.VMEM((rows, width), bf),
+        pltpu.VMEM((rows, width), bf),
+        pltpu.VMEM((rows, width), bf),
+        pltpu.VMEM((4, rows, width), bf),
+        pltpu.VMEM((4, 6, frame_rows, frame_rows), bf),
+        pltpu.VMEM((4, rows, local), bf),
+        pltpu.VMEM((rows, width), f32),
+        pltpu.VMEM((rows, width), f32),
+        pltpu.VMEM((rows, width), f32),
+        pltpu.VMEM((rows, width), f32),
+        pltpu.VMEM((2, rows, width), bf),
+        pltpu.VMEM((rows, width), bf),
+        pltpu.VMEM((rows, width), bf),
+        pltpu.VMEM((4, 32, width), bf),
+        pltpu.VMEM((4, 32, local), bf),
+        pltpu.VMEM((4, 32, width), bf),
+        pltpu.VMEM((4, 32, width), bf),
+        pltpu.VMEM((4, 32, width), bf),
+        pltpu.VMEM((4, 32, local), bf),
+        pltpu.VMEM((2, 2, 2, 2, 32, width), bf),
+        pltpu.VMEM((4, 2, 32, width), bf),
+        pltpu.VMEM((4, 2, 32, width), bf),
+        pltpu.VMEM((16, 32, span), bf),
+        pltpu.VMEM((2, HALF_SLOT, width), bf),
+        pltpu.VMEM((2, HALF_SLOT, width), bf),
+        pltpu.VMEM((8, rows, 32), bf),
+        pltpu.SemaphoreType.DMA((2, 4)),
+        pltpu.SemaphoreType.DMA((2, 4)),
+        pltpu.SemaphoreType.DMA((4,)),
+        pltpu.SemaphoreType.DMA((4,)),
+        pltpu.SemaphoreType.DMA((9, 9)),
+        pltpu.SemaphoreType.DMA((9, 9)),
+        pltpu.SemaphoreType.DMA((4,)),
+        pltpu.SemaphoreType.DMA((4,)),
+        pltpu.SemaphoreType.DMA((4,)),
+        pltpu.SemaphoreType.DMA((4,)),
+        pltpu.SemaphoreType.DMA((4, 4)),
+        pltpu.SemaphoreType.DMA((16,)),
+    ]
+    act, ing, grads = pl.pallas_call(
+        fused_kernel,
+        out_shape=(
+            jax.ShapeDtypeStruct((micro_count, HALF_SLOT, width), bf),
+            jax.ShapeDtypeStruct((micro_count, HALF_SLOT, width), bf),
+            jax.ShapeDtypeStruct((2, 2 * RANK, span), f32),
+        ),
+        in_specs=[vmem] * 6,
+        out_specs=(vmem, vmem, vmem),
+        scratch_shapes=scratch,
+        compiler_params=pltpu.CompilerParams(
+            collective_id=0, has_side_effects=True, vmem_limit_bytes=60 * 2**20
+        ),
+    )(tokens, cotangent, gain_one[None], gain_two[None], shard, adp)
+    grads = grads.reshape(micro_count, RANK, span)
+    hit = clip_adapter[None, :] == lax.broadcasted_iota(
+        jnp.int32, (rank_all // RANK, micro_count), 0
+    )
+    owner_grad = sum(
+        jnp.where(hit[:, m, None, None], grads[m][None], 0.0) for m in range(micro_count)
+    ).reshape(rank_all, span)
+    return (act[:, :shard_rows], ing[:, :shard_rows]) + adam(
+        owner_grad, adapters, moment_one, moment_two
+    )
+
+
+def layer(tokens, *others):
+    w_up = others[6]
+    sizes = lax.axis_size("dp"), lax.axis_size("mp")
+    frames_micro = tokens.shape[1] * sizes[0] * sizes[1] // FRAME
+    fits = (
+        sizes == (8, 4)
+        and tokens.shape[0] == 4
+        and 2 * tokens.shape[1] == FRAME
+        and frames_micro == CLIP_FRAMES
+        and w_up.shape == (tokens.shape[2] // 8, tokens.shape[2])
+    )
+    return (fused if fits else shards)(tokens, *others)
 
 
 def solution(mesh):
     spread = P(None, ("dp", "mp"))
     rows = P(None, ("dp", "mp"), None)
     return jax.shard_map(
-        shards,
+        layer,
         mesh=mesh,
         in_specs=(
             rows,

time: 602 us -> 162 us (0.27)
  waiting for transfers between devices: 384 us -> 0 us
  Pallas kernels: 0 us -> 146 us
  matrix products: 77.2 us -> 0 us
  local copies, waits for them, and re-layouts: 69.9 us -> 11.8 us
  blocking collectives: 25.6 us -> 0 us
  starting transfers between devices: 15.3 us -> 0 us
  between operations: 15.2 us -> 0.75 us
  other arithmetic: 9.93 us -> 2.18 us
    all_gather x7 -> x0, waiting for transfers between devices: 287 us -> none  [the longest x4 228 us: whole(): lax.all_gather(lax.all_gather(weight, first[0], axis=first[1], tiled=True...]
    pallas_call x0 -> x1, Pallas kernels: none -> 146 us  [fused(): pl.pallas_call(fused_kernel, out_shape=(jax.ShapeDtypeStruct((micro_count...]
    reduce_scatter x1 -> x0, waiting for transfers between devices: 77.8 us -> none  [shards(): lax.psum_scatter(dot(pick, grads), ('dp', 'mp'), scatter_dimension=1, til...]
    dot_general x38 -> x0, matrix products: 71.6 us -> none  [the longest x13 36 us: dot(): return jnp.dot(left, right, preferred_element_type=jnp.float32)]
    reshape x17 -> x1, local copies, waits for them, and re-layouts: 35.6 us -> 0.15 us  [fused(): w_qkv.reshape(w_qkv.shape[0], -1)]
    all_gather x2 -> x0, blocking collectives: 25.6 us -> none  [whole(): lax.all_gather(weight, first[0], axis=first[1], tiled=True)]
    all_to_all x4 -> x0, waiting for transfers between devices: 17.1 us -> none  [the longest x2 9.03 us: swap_back(): lax.all_to_all(rows.reshape(mine, FRAME, width), 'mp', split_axis=1, conc...]
    all_to_all x4 -> x0, starting transfers between devices: 14.8 us -> none  [the longest x2 7.76 us: swap(): lax.all_to_all(rows, 'mp', split_axis=0, concat_axis=1, axis_index_groups...]
  transfers between devices with their start and end apart: 12 -> 0, of which waited for: 9 -> 0; matrix products, arithmetic and copies ran while one was open for 15% -> 0% of each run, Pallas kernels for 0% -> 0%
where the time goes in v2:
time: 162 us; the launch traced here: 161 us
  Pallas kernels  146 us (90%)
  local copies, waits for them, and re-layouts  11.8 us (7%)
  other arithmetic  2.18 us (1%)
    pallas_call x1, Pallas kernels, fused(): pl.pallas_call(fused_kernel, out_shape=(jax.ShapeDtypeStruct((micro_count...  146 us
    unnamed x32, local copies, waits for them, and re-layouts  7.75 us

profile of v2, /device:TPU:0, one launch (start us, length us, event | category | flops | bytes accessed | tf_op | source)
XLA Modules:
  0.0 161.2 jit_solution(16616697103190897867)
XLA Ops:
  0.6 1.1 copy.26
  1.7 0.0 copy-start.9
  1.7 0.1 copy.27
  1.9 0.6 copy-done.9
  2.5 0.0 copy-start.7
  2.5 0.0 copy-start.8
  2.5 0.1 copy.25
  2.6 0.0 copy-start.1
  2.6 0.1 maximum_bitcast_fusion
  2.7 0.7 copy-done.7
  3.4 0.1 copy-done.8
  3.5 0.8 pad_maximum_fusion.shard_ref
  4.3 0.0 copy-done.1
  4.3 0.0 copy-start.2
  4.3 0.9 copy.28.tok_ref
  5.2 0.4 copy-done.2
  5.6 0.0 copy-start
  5.6 0.9 copy.29.cot_ref
  6.5 0.0 copy-done
  6.6 0.0 copy-start.12
  6.6 0.6 copy-done.12
  7.2 0.0 copy-start.10
  7.3 1.2 gather_fusion
  8.4 0.0 copy-done.10
  8.4 0.6 broadcast_in_dim.103.g1_ref
  9.0 0.1 copy-done.11
  9.1 0.6 broadcast_in_dim.104.g2_ref
  9.7 146.5 %shard_map.171 = (bf16[4,112,768]{2,1,0:T(8,128)(2,1)}, bf16[4,112,768]{2,1,0:T(8,128)(2,1)}, f32[2,32,384]{2,1,0:T(8,128)}) custom-call(bf16[4,98,768]{2,1,0:T(8,128)(2,1)} %copy.28.tok_ref, bf16[4,98,768]{2,1,0:T(8,128)(2,1)} %copy.29.cot_ref, f32[1,768]{1,0:T(1,128)} %broadcast_in_dim.103.g1_ref, f32[1,768]{1,0:T(1,128)} %broadcast_in_dim.104.g2_ref, ...), custom_call_target="tpu_custom_call" | custom-call | tf_op jit(solution)/shard_map/pallas_call | solution.py:870
  156.2 0.0 copy-start.5
  156.2 0.8 slice_bitcast_fusion.3
  157.0 0.1 iota_compare_fusion
  157.1 0.1 broadcast_in_dim.107
  157.2 0.1 broadcast_in_dim.108
  157.3 0.1 broadcast_in_dim.115
  157.3 0.1 broadcast_in_dim.116
  157.4 0.1 broadcast_in_dim.122
  157.5 0.1 broadcast_in_dim.123
  157.6 0.1 broadcast_in_dim.129
  157.7 0.1 broadcast_in_dim.130
  157.8 0.0 copy-done.6
  157.8 0.0 copy-done.5
  157.8 0.0 copy-start.4
  157.8 1.2 fusion.4
  159.0 0.0 copy-done.4
  159.0 0.0 copy-start.3
  159.0 1.1 copy.30
  160.1 0.0 copy-done.3
  160.1 1.1 copy.31
  (8 shorter events, 0.1 us)
Async XLA Ops:
  1.7 0.8 copy-start.9
  2.5 0.9 copy-start.7
  2.5 1.0 copy-start.8
  2.6 1.7 %copy-start.1 = (bf16[4,98,768]{2,0,1:T(4,128)(2,1)S(1)}, bf16[4,98,768]{2,0,1:T(4,128)(2,1)}, u32[]{:S(2)}) copy-start(bf16[4,98,768]{2,0,1:T(4,128)(2,1)} %param.12) | copy-start | bytes 1806340
  4.3 1.3 copy-start.2
  5.6 1.0 copy-start
  6.6 0.7 copy-start.12
  7.2 1.2 copy-start.10
  8.4 0.7 copy-start.11
  9.7 148.1 %copy-start.6 = (f32[128,384]{1,0:T(8,128)S(1)}, f32[128,384]{1,0:T(8,128)}, u32[]{:S(2)}) copy-start(f32[128,384]{1,0:T(8,128)} %param.23) | copy-start | bytes 589828
  156.2 1.6 copy-start.5
  157.8 1.2 copy-start.4
  159.0 1.1 copy-start.3

commit v3 on v2

--- a/solution.py
+++ b/solution.py
@@ -243,13 +243,16 @@
     cot_ref,
     g1_ref,
     g2_ref,
-    shard_ref,
-    adp_ref,
+    wq_ref,
+    wo_ref,
+    wu_ref,
+    wd_ref,
+    table_ref,
+    clip_ref,
     act_ref,
     ing_ref,
     gr_ref,
-    wa,
-    wf,
+    w,
     ad,
     ts,
     cs,
@@ -273,14 +276,17 @@
     ao,
     bu,
     an,
-    gq,
-    go,
     g16,
     gc,
     gs,
     rb,
     osend,
     isend,
+    own_act,
+    own_ing,
+    orecv,
+    irecv,
+    adp,
     smalls,
     zs,
     zr,
@@ -303,7 +309,7 @@
     h = lax.rem(z, 2)
     zp = z + 1 - 2 * h
     zn = 4
-    shard_rows = tok_ref.shape[1]
+    shard_rows = tok_ref.shape[0]
     rows = xf.shape[0]
     frame_rows = rows // 2
     width = xf.shape[1]
@@ -312,6 +318,18 @@
 
     def place(yy, xx, cc, zz):
         return ((yy * 2 + xx) * 2 + cc, zz)
+
+    def order(at_z, k):
+        upper = at_z // 2
+        near = at_z + upper * (3 - 2 * at_z)
+        swapped = jnp.where((near == 1) & (k < 2), 1 - k, k)
+        return swapped + upper * (3 - 2 * swapped)
+
+    def rank_of(at_z, block_z):
+        upper = at_z // 2
+        near = at_z + upper * (3 - 2 * at_z)
+        mirrored = block_z + upper * (3 - 2 * block_z)
+        return jnp.where((near == 1) & (mirrored < 2), 1 - mirrored, mirrored)
 
     barrier = pltpu.get_barrier_semaphore()
     for k in range(1, 16):
@@ -330,29 +348,33 @@
             device_id_type=MESH,
         )
 
-    wa[z, y, x, c] = shard_ref[0]
-    wf[z, 0, y, x, c] = shard_ref[1]
-    wf[z, 1, y, x, c] = shard_ref[2]
+    w[z, 0, y, x, c] = jnp.concatenate([wo_ref[...].T] + [wq_ref[i] for i in range(3)], axis=1)
+    span = table_ref.shape[1]
+    low_columns = pl.ds(pl.multiple_of(lax.rem(z, 2) * span, 128), span)
     for m in range(4):
-        ts[m, pl.ds(96, 16)] = jnp.zeros((16, width), jnp.bfloat16)
-        cs[m, pl.ds(96, 16)] = jnp.zeros((16, width), jnp.bfloat16)
-        ts[m, pl.ds(0, shard_rows)] = tok_ref[m]
-        cs[m, pl.ds(0, shard_rows)] = cot_ref[m]
-    span = adp_ref.shape[2]
-    low_columns = pl.ds(pl.multiple_of(lax.rem(z, 2) * span, 128), span)
-    ad[y, x, c, z // 2, :, low_columns] = adp_ref[h]
-
-    def part(s, zk, yy, xx, cc, first, count):
-        if s == 0:
-            return wa.at[zk, yy, xx, cc, pl.ds(first, count), :]
-        if s == 1:
-            return wf.at[zk, :, yy, xx, cc, pl.ds(first, count), :]
-        return ad.at[yy, xx, cc, :, pl.ds(first, count), :]
-
-    def move(s, k, what):
-        full = 32 if s == 2 else 96
+        clip = jnp.full((RANK, span), clip_ref[m])
+        chosen = jnp.zeros((RANK, span), jnp.float32)
+        for a in range(table_ref.shape[0] // RANK):
+            chosen = jnp.where(clip == a, table_ref[a * RANK : (a + 1) * RANK], chosen)
+        adp[m // 2, pl.ds((m % 2) * RANK, RANK)] = chosen.astype(jnp.bfloat16)
+    ad[y, x, c, z // 2, :, low_columns] = adp[h]
+
+    def stage(dst, src):
+        for m in range(4):
+            dst[m, pl.ds(96, 16)] = jnp.zeros((16, width), jnp.bfloat16)
+            dst[m, pl.ds(0, shard_rows)] = src[:, m, :]
+
+    def part(kind, zk, yy, xx, cc, first, count):
+        return w.at[zk, kind, yy, xx, cc, pl.ds(first, count), :]
+
+    def phase(q):
+        if isinstance(q, int):
+            return (0, q) if q < 4 else (1 + q % 2, (q - 4) // 2)
+        return 1 + lax.rem(q, 2), (q - 4) // 2
+
+    def move(q, what):
+        full = 32 if q is None else 96
         n = full // 2
-        zk = lax.rem(z + k, zn)
         every = pl.ds(0, 2)
         args, target = {
             X1: ((y, x, c, 0, n), (y, 1 - x, c)),
@@ -365,50 +387,58 @@
             C2A: ((1 - y, every, c, 0, n), (y, x, 1 - c)),
             C2B: ((every, 1 - x, c, n, n), (y, x, 1 - c)),
         }[what]
-        ref = part(s, zk, *args)
-        index = s * 4 + k
+        if q is None:
+            yy, xx, cc, first, count = args
+            ref = ad.at[yy, xx, cc, :, pl.ds(first, count), :]
+            index = 12
+        else:
+            kind, k = phase(q)
+            ref = part(kind, order(z, k), *args)
+            index = q
         return remote(ref, ref, ss.at[index, what], rs.at[index, what], place(*target, z))
 
-    def z_move(s, j):
-        ref = part(s, z, y, x, c, 0, 96)
-        return remote(ref, ref, zs.at[s, j], zr.at[s, j], (dp, lax.rem(z + zn - j, zn)))
+    def z_move(q):
+        kind, k = phase(q)
+        ref = part(kind, z, y, x, c, 0, 96)
+        other = order(z, k)
+        return remote(ref, ref, zs.at[kind, k], zr.at[kind, rank_of(other, z)], (dp, other))
+
+    def z_wait(q):
+        kind, k = phase(q)
+        ref = part(kind, z, y, x, c, 0, 96)
+        remote(ref, ref, zs.at[kind, k], zr.at[kind, k], (dp, zp)).wait_recv()
 
     def ad_move(j):
         other = lax.rem(z + zn - j, zn)
         dst = ad.at[y, x, c, z // 2, :, low_columns]
-        return remote(adp_ref.at[lax.rem(other, 2)], dst, azs.at[j], azr.at[j], (dp, other))
-
-    def t1(s, k):
-        if s < 2:
-            if isinstance(k, int):
-                if k:
-                    z_move(s, k).wait_recv()
-            else:
-
-                @pl.when(k > 0)
-                def _():
-                    z_move(s, k).wait_recv()
-
+        return remote(adp.at[lax.rem(other, 2)], dst, azs.at[j], azr.at[j], (dp, other))
+
+    def t1(q):
+        if isinstance(q, int):
+            if q is not None and phase(q)[1]:
+                z_wait(q)
+        elif q is not None:
+            z_wait(q)
         for what in (X1, Y1, C0):
-            move(s, k, what).start()
-
-    def t2(s, k):
-        move(s, k, X1).wait_recv()
-        move(s, k, Y2).start()
-        move(s, k, Y1).wait_recv()
-        move(s, k, X2).start()
-        move(s, k, C1A).start()
-        move(s, k, C1B).start()
-
-    def t3(s, k):
-        move(s, k, Y2).wait_recv()
-        move(s, k, C2A).start()
-        move(s, k, X2).wait_recv()
-        move(s, k, C2B).start()
-
-    def ready(s, k):
+            move(q, what).start()
+
+    def t2(q):
+        move(q, X1).wait_recv()
+        move(q, Y2).start()
+        move(q, Y1).wait_recv()
+        move(q, X2).start()
+        move(q, C1A).start()
+        move(q, C1B).start()
+
+    def t3(q):
+        move(q, Y2).wait_recv()
+        move(q, C2A).start()
+        move(q, X2).wait_recv()
+        move(q, C2B).start()
+
+    def ready(q):
         for what in (C0, C1A, C1B, C2A, C2B):
-            move(s, k, what).wait_recv()
+            move(q, what).wait_recv()
 
     tok_move = remote(
         ts.at[pl.ds(2 - 2 * h, 2)], tr, ps.at[0], pr.at[0], (dp, zp)
@@ -417,28 +447,49 @@
         cs.at[pl.ds(2 - 2 * h, 2)], cr, ps.at[1], pr.at[1], (dp, zp)
     )
     act_move = remote(
-        osend, act_ref.at[pl.ds(2 * h, 2)], ps.at[2], pr.at[2], (dp, zp)
+        osend, orecv, ps.at[2], pr.at[2], (dp, zp)
     )
     ing_move = remote(
-        isend, ing_ref.at[pl.ds(2 * h, 2)], ps.at[3], pr.at[3], (dp, zp)
+        isend, irecv, ps.at[3], pr.at[3], (dp, zp)
     )
 
     pl.semaphore_wait(barrier, 16)
+    t1(0)
     for j in range(1, 4):
         ad_move(j).start()
+    for j in range(1, 4):
+        z_move(j).start()
+    w[z, 1, y, x, c] = wu_ref[...]
+    t1(4)
+    stage(ts, tok_ref)
     tok_move.start()
-    t1(0, 0)
-    for j in range(1, 4):
-        z_move(0, j).start()
-    cot_move.start()
-    for j in range(1, 4):
-        z_move(1, j).start()
+    w[z, 2, y, x, c] = wd_ref[...]
+    t2(0)
+    t1(1)
     for j in range(1, 4):
         ad_move(j).wait_recv()
-    t1(2, 0)
-    t1(0, 1)
-    t2(0, 0)
-    t2(2, 0)
+    t1(None)
+    t2(1)
+    t1(2)
+    t2(None)
+    t3(0)
+    z_move(6).start()
+    z_move(7).start()
+    t2(2)
+    t1(3)
+    t3(1)
+    t3(None)
+    stage(cs, cot_ref)
+    cot_move.start()
+    t2(3)
+    t2(4)
+    t3(2)
+    z_move(8).start()
+    z_move(9).start()
+    t1(5)
+    t3(3)
+    z_move(10).start()
+    z_move(11).start()
 
     def dot(left, right):
         return jnp.dot(left, right, preferred_element_type=jnp.float32)
@@ -460,7 +511,7 @@
     def low(values):
         return jnp.where(mask, values, 0.0).astype(jnp.bfloat16)
 
-    def tiles(body, step=16):
+    def tiles(body, step=416):
         @pl.loop(0, rows // step)
         def _(t):
             body(pl.ds(pl.multiple_of(t * step, step), step))
@@ -485,7 +536,7 @@
         return g16.at[g // 8, (g // 4) % 2, (g // 2) % 2, g % 2]
 
     def attn_block(zk):
-        return wa[zk].reshape(width, width)
+        return w[zk, 0].reshape(width, width)
 
     def halves(f):
         own = pl.ds(pl.multiple_of(f * frame_rows + h * HALF_PITCH, 8), HALF_PITCH)
@@ -498,18 +549,25 @@
             dst[own] = own_slots[2 * h + f][:HALF_PITCH].astype(jnp.float32)
             dst[other] = other_slots[f][:HALF_PITCH].astype(jnp.float32)
 
+    def give(dst, own, received):
+        for f in range(2):
+            first, second = own[f, pl.ds(0, shard_rows)], received[f, pl.ds(0, shard_rows)]
+            dst[:, f, :] = jnp.where(h == 0, first, second)
+            dst[:, 2 + f, :] = jnp.where(h == 0, second, first)
+
     tok_move.wait_recv()
     join(xf, ts, tr)
 
     def first_norm(at):
         values = xf[at]
         unit, _ = norm_parts(values)
-        n1[at] = (unit * g1_ref[...]).astype(jnp.bfloat16)
+        n1[at] = (unit * g1_ref[...].reshape(1, width)).astype(jnp.bfloat16)
         mid[at] = values
 
     tiles(first_norm)
-    t3(2, 0)
-    ready(2, 0)
+    ready(None)
+    for k in range(4):
+        ready(k)
     for k in range(4):
         bq[k] = jnp.concatenate(
             [jnp.zeros((32, local), jnp.bfloat16)]
@@ -528,7 +586,7 @@
     LOW_QKV, LOW_OUT, LOW_UP, LOW_DOWN, THR_DOWN, THR_UP, THR_OUT, THR_QKV = range(8)
 
     def attention(i, out_low):
-        zk = lax.rem(z + i, zn)
+        zk = order(z, i)
         block = attn_block(zk)
         proj[zk] = (dot(n1[...], block) + dot(smalls[LOW_QKV], bq[zk])).astype(jnp.bfloat16)
         for f in range(2):
@@ -551,33 +609,31 @@
         return out_low + dot_t(gathered, ao[zk])
 
     def attention_step(i, out_low):
-        @pl.when(i < 2)
+        @pl.when(i == 1)
         def _():
-            t1(0, i + 2)
-
-        @pl.when(i >= 2)
+            t1(6)
+            t2(5)
+
+        @pl.when(i == 2)
         def _():
-            t1(1, i - 2)
-
-        @pl.when(i < 3)
-        def _():
-            t2(0, i + 1)
+            t3(4)
 
         @pl.when(i == 3)
         def _():
-            t2(1, 0)
-
-        t3(0, i)
-        ready(0, i)
+            t1(7)
+            t2(6)
+
         return attention(i, out_low)
 
     out_low = lax.fori_loop(0, 4, attention_step, jnp.zeros((rows, 32), jnp.float32))
+    t3(5)
+    ready(4)
     smalls[LOW_OUT] = low(out_low)
     mid[...] += dot(smalls[LOW_OUT], group(5))
 
     def second_norm(at):
         unit, _ = norm_parts(mid[at])
-        n2[at] = (unit * g2_ref[...]).astype(jnp.bfloat16)
+        n2[at] = (unit * g2_ref[...].reshape(1, width)).astype(jnp.bfloat16)
 
     tiles(second_norm)
     cot_move.wait_recv()
@@ -586,15 +642,22 @@
     smalls[LOW_UP] = low(dot_t(n2[...], group(6)))
     smalls[THR_DOWN] = low(dot_t(dyb[...], group(15)))
     group_ref(15)[...] = jnp.zeros((32, width), jnp.bfloat16)
+    t1(8)
+    t2(7)
     acc[...] = mid[...]
     dn[...] = jnp.zeros_like(dn)
 
     def feed(i, lows):
         down_low, up_back = lows
-        zk = lax.rem(z + i, zn)
-        up = wf[zk, 0].reshape(width, width)
-        down = wf[zk, 1].reshape(width, width)
-        tmp[...] = dot(n2[...], up) + dot(smalls[LOW_UP], bu[zk])
+        zk = order(z, i)
+        q = 4 + 2 * i
+
+        @pl.when((i > 0) & (i < 3))
+        def _():
+            t1(q + 3)
+            t2(q + 2)
+
+        tmp[...] = dot(n2[...], w[zk, 1].reshape(width, width)) + dot(smalls[LOW_UP], bu[zk])
 
         def gate(at):
             hidden = tmp[at]
@@ -605,11 +668,26 @@
 
         tiles(gate)
         active = buf[0]
-        acc[...] += dot_t(active, down)
+
+        @pl.when(i > 0)
+        def _():
+            t3(q + 1)
+
+        @pl.when(i == 1)
+        def _():
+            t1(q + 4)
+
+        @pl.when((i > 0) & (i < 3))
+        def _():
+            t2(q + 3)
+
+        ready(q + 1)
+        down = w[zk, 2].reshape(width, width)
         tmp[...] = tmp[...] * (dot(dyb[...], down) + dot(smalls[THR_DOWN], an[zk]))
         buf[1] = tmp[...].astype(jnp.bfloat16)
         d_hidden = buf[1]
-        dn[...] += dot_t(d_hidden, up)
+        dn[...] += dot_t(d_hidden, w[zk, 1].reshape(width, width))
+        acc[...] += dot_t(active, down)
         gu = 7 + zk
         ga = 11 + zk
         g16[gu // 8, lax.rem(gu // 4, 2), lax.rem(gu // 2, 2), lax.rem(gu, 2)] = t_dot(
@@ -618,23 +696,18 @@
         g16[ga // 8, lax.rem(ga // 4, 2), lax.rem(ga // 2, 2), lax.rem(ga, 2)] = t_dot(
             smalls[THR_DOWN], active
         ).astype(jnp.bfloat16)
-        return down_low + dot_t(active, an[zk]), up_back + dot_t(d_hidden, bu[zk])
-
-    def feed_step(i, lows):
-        @pl.when(i < 2)
-        def _():
-            t1(1, i + 2)
+        down_low = down_low + dot_t(active, an[zk])
+        up_back = up_back + dot_t(d_hidden, bu[zk])
 
         @pl.when(i < 3)
         def _():
-            t2(1, i + 1)
-
-        t3(1, i)
-        ready(1, i)
-        return feed(i, lows)
+            t3(q + 2)
+            ready(q + 2)
+
+        return down_low, up_back
 
     empty = jnp.zeros((rows, 32), jnp.float32)
-    down_low, up_back = lax.fori_loop(0, 4, feed_step, (empty, empty))
+    down_low, up_back = lax.fori_loop(0, 4, feed, (empty, empty))
     smalls[LOW_DOWN] = low(down_low)
     smalls[THR_UP] = low(up_back)
     group_ref(15)[...] = t_dot(smalls[LOW_DOWN], dyb[...]).astype(jnp.bfloat16)
@@ -676,7 +749,7 @@
     acc[...] += dot(smalls[LOW_DOWN], group(15))
 
     def second_back(at):
-        value = dyb[at].astype(jnp.float32) + norm_back(mid[at], g2_ref[...], dn[at])
+        value = dyb[at].astype(jnp.float32) + norm_back(mid[at], g2_ref[...].reshape(1, width), dn[at])
         dn[at] = value
         dbr[at] = value.astype(jnp.bfloat16)
 
@@ -684,15 +757,20 @@
     for f in range(2):
         own, other = halves(f)
         osend[f, pl.ds(0, HALF_PITCH)] = acc[other].astype(jnp.bfloat16)
-        act_ref[2 * h + f, pl.ds(0, HALF_PITCH)] = acc[own].astype(jnp.bfloat16)
+        own_act[f] = acc[own].astype(jnp.bfloat16)
     act_move.start()
     smalls[THR_OUT] = low(dot_t(dbr[...], group(5)))
     group_ref(5)[...] = t_dot(smalls[LOW_OUT], dbr[...]).astype(jnp.bfloat16)
-    dpj[:, 0:local] = jnp.zeros((rows, local), jnp.bfloat16)
+    for k in range(4):
+        dpj[k, :, 0:local] = jnp.zeros((rows, local), jnp.bfloat16)
     acc[...] = jnp.zeros_like(acc)
 
     spread_out(3)
     spread_out(2)
+    group_ref(4)[...] = jnp.concatenate(
+        [t_dot(smalls[THR_OUT], att[k]).astype(jnp.bfloat16) for k in range(4)], axis=1
+    )
+    core_move(1).start()
 
     def attention_back(zk, qkv_back):
         block = attn_block(zk)
@@ -700,7 +778,11 @@
             jnp.bfloat16
         )
         buf[0, :, 0:local] = d_att
-        go[zk] = t_dot(smalls[THR_OUT], att[zk]).astype(jnp.bfloat16)
+
+        @pl.when(zk == 1)
+        def _():
+            spread_out(1)
+
         for f in range(2):
             at = pl.ds(f * frame_rows, frame_rows)
             for head in range(3):
@@ -716,42 +798,41 @@
                 inner = jnp.sum(wide * d_soft, axis=0, keepdims=True)
                 d_scores = (wide * (d_soft - inner)).astype(jnp.bfloat16)
                 d_keys = dot(d_scores, q) * scale
-                d_queries = t_dot(d_scores, k) * scale
-                dpj[at, first : first + HEAD] = d_queries.astype(jnp.bfloat16)
-                dpj[at, first + local : first + local + HEAD] = d_keys.astype(jnp.bfloat16)
-                dpj[at, first + 2 * local : first + 2 * local + HEAD] = d_values.astype(
+                d_queries = t_dot(k, d_scores).T * scale
+                dpj[zk, at, first : first + HEAD] = d_queries.astype(jnp.bfloat16)
+                dpj[zk, at, first + local : first + local + HEAD] = d_keys.astype(jnp.bfloat16)
+                dpj[zk, at, first + 2 * local : first + 2 * local + HEAD] = d_values.astype(
                     jnp.bfloat16
                 )
-        d_projected = dpj[...]
-        gq[zk] = t_dot(smalls[LOW_QKV], d_projected).astype(jnp.bfloat16)
+        d_projected = dpj[zk]
         acc[...] += dot_t(d_projected, block)
         return qkv_back + dot_t(d_projected, bq[zk])
 
     qkv_back = lax.fori_loop(0, 4, attention_back, empty)
     smalls[THR_QKV] = low(qkv_back)
-    group_ref(0)[...] = t_dot(smalls[THR_QKV], n1[...]).astype(jnp.bfloat16)
-    for i in range(3):
-        first = (1 + i) * local
-        group_ref(1 + i)[...] = jnp.concatenate(
-            [gq[k][:, first : first + local] for k in range(4)], axis=1
-        )
-    group_ref(4)[...] = jnp.concatenate([go[k] for k in range(4)], axis=1)
-    core_move(1).start()
-    core_move(0).start()
-
     acc[...] += dot(smalls[THR_QKV], group(0))
 
     def first_back(at):
-        acc[at] = dn[at] + norm_back(xf[at], g1_ref[...], acc[at])
+        acc[at] = dn[at] + norm_back(xf[at], g1_ref[...].reshape(1, width), acc[at])
 
     tiles(first_back)
     for f in range(2):
         own, other = halves(f)
         isend[f, pl.ds(0, HALF_PITCH)] = acc[other].astype(jnp.bfloat16)
-        ing_ref[2 * h + f, pl.ds(0, HALF_PITCH)] = acc[own].astype(jnp.bfloat16)
+        own_ing[f] = acc[own].astype(jnp.bfloat16)
     ing_move.start()
-    spread_out(1)
+    group_ref(0)[...] = t_dot(smalls[THR_QKV], n1[...]).astype(jnp.bfloat16)
+    parts = [t_dot(smalls[LOW_QKV], dpj[k]).astype(jnp.bfloat16) for k in range(4)]
+    for i in range(3):
+        first = (1 + i) * local
+        group_ref(1 + i)[...] = jnp.concatenate(
+            [parts[k][:, first : first + local] for k in range(4)], axis=1
+        )
+    core_move(0).start()
     spread_out(0)
+
+    act_move.wait_recv()
+    give(act_ref, own_act, orecv)
 
     for slot in range(1, 16):
         remote(rb.at[slot], rb.at[slot], us.at[0, 0], ur.at[slot], (dp, zp)).wait_recv()
@@ -760,7 +841,17 @@
         for slot in range(16):
             if slot % 2 == parity:
                 total = total + rb[slot].astype(jnp.float32)
-        gr_ref[lax.rem(h + parity, 2)] = total
+        first = lax.rem(h + parity, 2)
+        for a in range(table_ref.shape[0] // RANK):
+            chosen = [
+                jnp.where(
+                    jnp.full((RANK, span), clip_ref[2 * first + i]) == a,
+                    total[i * RANK : (i + 1) * RANK],
+                    0.0,
+                )
+                for i in range(2)
+            ]
+            gr_ref[first, pl.ds(a * RANK, RANK)] = chosen[0] + chosen[1]
     for yx in range(4):
         core_move(yx).wait_send()
         for zz in range(4):
@@ -774,19 +865,23 @@
     cot_move.wait_send()
     for j in range(1, 4):
         ad_move(j).wait_send()
-        z_move(0, j).wait_send()
-        z_move(1, j).wait_send()
-
-    @pl.loop(0, 4)
-    def _(k):
+
+    for q in (1, 2, 3, 6, 7, 8, 9, 10, 11):
+        z_move(q).wait_send()
+    for q in range(4):
         for what in range(9):
-            move(0, k, what).wait_send()
-            move(1, k, what).wait_send()
+            move(q, what).wait_send()
+
+    @pl.loop(4, 12)
+    def _(q):
+        for what in range(9):
+            move(q, what).wait_send()
 
     for what in range(9):
-        move(2, 0, what).wait_send()
-    act_move.wait()
+        move(None, what).wait_send()
+    act_move.wait_send()
     ing_move.wait()
+    give(ing_ref, own_ing, irecv)
 
 
 def fused(
@@ -805,23 +900,13 @@
 ):
     micro_count, shard_rows, width = tokens.shape
     rank_all, span = adapters.shape
-    shard = jnp.stack(
-        [
-            jnp.concatenate([w_out.T, w_qkv.reshape(w_qkv.shape[0], -1)], axis=1),
-            w_up,
-            w_down.T,
-        ]
-    )
-    picked = adapters.astype(jnp.bfloat16).reshape(rank_all // RANK, RANK, span)[clip_adapter]
-    adp = picked.reshape(2, 2 * RANK, span)
     rows = 4 * HALF_PITCH
     frame_rows = 2 * HALF_PITCH
     local = width // 4
     bf, f32 = jnp.bfloat16, jnp.float32
     vmem = pl.BlockSpec(memory_space=pltpu.VMEM)
     scratch = [
-        pltpu.VMEM((4, 2, 2, 2, 96, width), bf),
-        pltpu.VMEM((4, 2, 2, 2, 2, 96, width), bf),
+        pltpu.VMEM((4, 3, 2, 2, 2, 96, width), bf),
         pltpu.VMEM((2, 2, 2, 2, 32, width), bf),
         pltpu.VMEM((4, HALF_SLOT, width), bf),
         pltpu.VMEM((4, HALF_SLOT, width), bf),
@@ -840,26 +925,29 @@
         pltpu.VMEM((rows, width), f32),
         pltpu.VMEM((2, rows, width), bf),
         pltpu.VMEM((rows, width), bf),
-        pltpu.VMEM((rows, width), bf),
+        pltpu.VMEM((4, rows, width), bf),
         pltpu.VMEM((4, 32, width), bf),
         pltpu.VMEM((4, 32, local), bf),
         pltpu.VMEM((4, 32, width), bf),
         pltpu.VMEM((4, 32, width), bf),
-        pltpu.VMEM((4, 32, width), bf),
-        pltpu.VMEM((4, 32, local), bf),
         pltpu.VMEM((2, 2, 2, 2, 32, width), bf),
         pltpu.VMEM((4, 2, 32, width), bf),
         pltpu.VMEM((4, 2, 32, width), bf),
         pltpu.VMEM((16, 32, span), bf),
         pltpu.VMEM((2, HALF_SLOT, width), bf),
         pltpu.VMEM((2, HALF_SLOT, width), bf),
+        pltpu.VMEM((2, HALF_PITCH, width), bf),
+        pltpu.VMEM((2, HALF_PITCH, width), bf),
+        pltpu.VMEM((2, HALF_SLOT, width), bf),
+        pltpu.VMEM((2, HALF_SLOT, width), bf),
+        pltpu.VMEM((2, 32, span), bf),
         pltpu.VMEM((8, rows, 32), bf),
-        pltpu.SemaphoreType.DMA((2, 4)),
-        pltpu.SemaphoreType.DMA((2, 4)),
+        pltpu.SemaphoreType.DMA((3, 4)),
+        pltpu.SemaphoreType.DMA((3, 4)),
         pltpu.SemaphoreType.DMA((4,)),
         pltpu.SemaphoreType.DMA((4,)),
-        pltpu.SemaphoreType.DMA((9, 9)),
-        pltpu.SemaphoreType.DMA((9, 9)),
+        pltpu.SemaphoreType.DMA((13, 9)),
+        pltpu.SemaphoreType.DMA((13, 9)),
         pltpu.SemaphoreType.DMA((4,)),
         pltpu.SemaphoreType.DMA((4,)),
         pltpu.SemaphoreType.DMA((4,)),
@@ -870,26 +958,30 @@
     act, ing, grads = pl.pallas_call(
         fused_kernel,
         out_shape=(
-            jax.ShapeDtypeStruct((micro_count, HALF_SLOT, width), bf),
-            jax.ShapeDtypeStruct((micro_count, HALF_SLOT, width), bf),
-            jax.ShapeDtypeStruct((2, 2 * RANK, span), f32),
+            jax.ShapeDtypeStruct((shard_rows, micro_count, width), bf),
+            jax.ShapeDtypeStruct((shard_rows, micro_count, width), bf),
+            jax.ShapeDtypeStruct((2, rank_all, span), f32),
         ),
-        in_specs=[vmem] * 6,
+        in_specs=[vmem] * 9 + [pl.BlockSpec(memory_space=pltpu.SMEM)],
         out_specs=(vmem, vmem, vmem),
         scratch_shapes=scratch,
         compiler_params=pltpu.CompilerParams(
             collective_id=0, has_side_effects=True, vmem_limit_bytes=60 * 2**20
         ),
-    )(tokens, cotangent, gain_one[None], gain_two[None], shard, adp)
-    grads = grads.reshape(micro_count, RANK, span)
-    hit = clip_adapter[None, :] == lax.broadcasted_iota(
-        jnp.int32, (rank_all // RANK, micro_count), 0
-    )
-    owner_grad = sum(
-        jnp.where(hit[:, m, None, None], grads[m][None], 0.0) for m in range(micro_count)
-    ).reshape(rank_all, span)
-    return (act[:, :shard_rows], ing[:, :shard_rows]) + adam(
-        owner_grad, adapters, moment_one, moment_two
+    )(
+        tokens.transpose(1, 0, 2),
+        cotangent.transpose(1, 0, 2),
+        gain_one,
+        gain_two,
+        w_qkv.transpose(1, 0, 2),
+        w_out,
+        w_up,
+        w_down.T,
+        adapters,
+        clip_adapter,
+    )
+    return (act.transpose(1, 0, 2), ing.transpose(1, 0, 2)) + adam(
+        grads[0] + grads[1], adapters, moment_one, moment_two
     )
 
 

time: 162 us -> 121 us (0.75)
  Pallas kernels: 146 us -> 116 us
  local copies, waits for them, and re-layouts: 11.8 us -> 2.12 us
    pallas_call x1, Pallas kernels: 146 us -> 116 us  [fused(): pl.pallas_call(fused_kernel, out_shape=(jax.ShapeDtypeStruct((shard_rows,...]
    unnamed x32 -> x12, local copies, waits for them, and re-layouts: 7.75 us -> 2.12 us
    broadcast_in_dim x12 -> x0, local copies, waits for them, and re-layouts: 2.66 us -> none  [the longest x10 1.5 us: fused(): jnp.where(hit[:, m, None, None], grads[m][None], 0.0)]
where the time goes in v3:
time: 121 us
  Pallas kernels  116 us (96%)
  local copies, waits for them, and re-layouts  2.12 us (2%)
  other arithmetic  2.03 us (2%)
    pallas_call x1, Pallas kernels, fused(): pl.pallas_call(fused_kernel, out_shape=(jax.ShapeDtypeStruct((shard_rows,...  116 us

profile of v3, /device:TPU:0, one launch (start us, length us, event | category | flops | bytes accessed | tf_op | source)
XLA Modules:
  0.0 121.0 jit_solution(10035063343805243831)
XLA Ops:
  0.6 0.0 copy-start
  0.6 0.0 copy-start.3
  0.7 0.0 copy-start.4
  0.7 116.1 %shard_map.171 = (bf16[98,4,768]{2,1,0:T(4,128)(2,1)}, bf16[98,4,768]{2,1,0:T(4,128)(2,1)}, f32[2,128,384]{2,1,0:T(8,128)}) custom-call(bf16[98,4,768]{2,1,0:T(4,128)(2,1)} %bitcast.11, bf16[98,4,768]{2,1,0:T(4,128)(2,1)} %bitcast.12, f32[768]{0:T(1024)} %g1_ref.1, f32[768]{0:T(1024)} %g2_ref.1, bf16[3,96,192]{2,1,0:T(8,128)(2,1)} %bitcast.13, ...), custom_call_target="tpu_custom_call" | custom-call | tf_op jit(solution)/shard_map/pallas_call | solution.py:958
  116.8 0.0 copy-done
  116.8 0.0 copy-done.3
  116.8 0.0 copy-done.4
  116.8 0.0 copy-start.2
  116.8 2.0 %fusion.1 = (bf16[128,384]{1,0:T(8,128)(2,1)}, f32[128,384]{1,0:T(8,128)}, f32[128,384]{1,0:T(8,128)}, f32[128,384]{1,0:T(8,128)}, f32[128,384]{1,0:T(8,128)}) fusion(f32[128,384]{1,0:T(8,128)S(1)} %copy-done, f32[128,384]{1,0:T(8,128)S(1)} %copy-done.3, f32[128,384]{1,0:T(8,128)S(1)} %copy-done.4, f32[2,128,384]{2,1,0:T(8,128)} %get-tuple-element.12), kind=kLoop, calls=%fused_computation.5 | loop fusion | flops 786432 | bytes 1867776 | tf_op jit(solution)/shard_map/convert_element_type | solution.py:67
  118.9 0.0 copy-done.2
  118.9 0.0 copy-start.1
  118.9 0.8 copy.21
  119.7 0.5 copy-done.1
  120.2 0.8 copy.22
Async XLA Ops:
  0.6 116.2 %copy-start = (f32[128,384]{1,0:T(8,128)S(1)}, f32[128,384]{1,0:T(8,128)}, u32[]{:S(2)}) copy-start(f32[128,384]{1,0:T(8,128)} %table_ref.1) | copy-start | bytes 589828
  0.6 116.2 %copy-start.3 = (f32[128,384]{1,0:T(8,128)S(1)}, f32[128,384]{1,0:T(8,128)}, u32[]{:S(2)}) copy-start(f32[128,384]{1,0:T(8,128)} %param.22) | copy-start | bytes 589828
  0.7 116.2 %copy-start.4 = (f32[128,384]{1,0:T(8,128)S(1)}, f32[128,384]{1,0:T(8,128)}, u32[]{:S(2)}) copy-start(f32[128,384]{1,0:T(8,128)} %param.23) | copy-start | bytes 589828
  116.8 2.0 %copy-start.2 = (bf16[98,4,768]{2,1,0:T(4,128)(2,1)S(1)}, bf16[98,4,768]{2,1,0:T(4,128)(2,1)}, u32[]{:S(2)}) copy-start(bf16[98,4,768]{2,1,0:T(4,128)(2,1)} %get-tuple-element.10) | copy-start | bytes 1806340
  118.9 1.3 %copy-start.1 = (bf16[98,4,768]{2,1,0:T(4,128)(2,1)S(1)}, bf16[98,4,768]{2,1,0:T(4,128)(2,1)}, u32[]{:S(2)}) copy-start(bf16[98,4,768]{2,1,0:T(4,128)(2,1)} %get-tuple-element.11) | copy-start | bytes 1806340

commit v4 on v3

--- a/solution.py
+++ b/solution.py
@@ -1,3 +1,4 @@
+import functools
 import math
 
 import jax
@@ -449,9 +450,9 @@
     act_move = remote(
         osend, orecv, ps.at[2], pr.at[2], (dp, zp)
     )
-    ing_move = remote(
-        isend, irecv, ps.at[3], pr.at[3], (dp, zp)
-    )
+    ing_moves = [
+        remote(isend.at[f], irecv.at[f], ps.at[3 + f], pr.at[3 + f], (dp, zp)) for f in range(2)
+    ]
 
     pl.semaphore_wait(barrier, 16)
     t1(0)
@@ -668,6 +669,11 @@
 
         tiles(gate)
         active = buf[0]
+        down_low = down_low + dot_t(active, an[zk])
+        ga = 11 + zk
+        g16[ga // 8, lax.rem(ga // 4, 2), lax.rem(ga // 2, 2), lax.rem(ga, 2)] = t_dot(
+            smalls[THR_DOWN], active
+        ).astype(jnp.bfloat16)
 
         @pl.when(i > 0)
         def _():
@@ -689,14 +695,9 @@
         dn[...] += dot_t(d_hidden, w[zk, 1].reshape(width, width))
         acc[...] += dot_t(active, down)
         gu = 7 + zk
-        ga = 11 + zk
         g16[gu // 8, lax.rem(gu // 4, 2), lax.rem(gu // 2, 2), lax.rem(gu, 2)] = t_dot(
             smalls[LOW_UP], d_hidden
         ).astype(jnp.bfloat16)
-        g16[ga // 8, lax.rem(ga // 4, 2), lax.rem(ga // 2, 2), lax.rem(ga, 2)] = t_dot(
-            smalls[THR_DOWN], active
-        ).astype(jnp.bfloat16)
-        down_low = down_low + dot_t(active, an[zk])
         up_back = up_back + dot_t(d_hidden, bu[zk])
 
         @pl.when(i < 3)
@@ -744,12 +745,14 @@
     core_move(3).start()
     core_move(2).start()
 
-    dn[...] += dot(smalls[THR_UP], group(6))
     group_ref(6)[...] = t_dot(smalls[THR_UP], n2[...]).astype(jnp.bfloat16)
     acc[...] += dot(smalls[LOW_DOWN], group(15))
 
     def second_back(at):
-        value = dyb[at].astype(jnp.float32) + norm_back(mid[at], g2_ref[...].reshape(1, width), dn[at])
+        grad = dn[at] + dot(smalls[THR_UP, at], group(6))
+        value = dyb[at].astype(jnp.float32) + norm_back(
+            mid[at], g2_ref[...].reshape(1, width), grad
+        )
         dn[at] = value
         dbr[at] = value.astype(jnp.bfloat16)
 
@@ -810,17 +813,18 @@
 
     qkv_back = lax.fori_loop(0, 4, attention_back, empty)
     smalls[THR_QKV] = low(qkv_back)
-    acc[...] += dot(smalls[THR_QKV], group(0))
 
     def first_back(at):
-        acc[at] = dn[at] + norm_back(xf[at], g1_ref[...].reshape(1, width), acc[at])
+        grad = acc[at] + dot(smalls[THR_QKV, at], group(0))
+        acc[at] = dn[at] + norm_back(xf[at], g1_ref[...].reshape(1, width), grad)
 
     tiles(first_back)
     for f in range(2):
         own, other = halves(f)
         isend[f, pl.ds(0, HALF_PITCH)] = acc[other].astype(jnp.bfloat16)
         own_ing[f] = acc[own].astype(jnp.bfloat16)
-    ing_move.start()
+    for f in range(2):
+        ing_moves[f].start()
     group_ref(0)[...] = t_dot(smalls[THR_QKV], n1[...]).astype(jnp.bfloat16)
     parts = [t_dot(smalls[LOW_QKV], dpj[k]).astype(jnp.bfloat16) for k in range(4)]
     for i in range(3):
@@ -880,8 +884,19 @@
     for what in range(9):
         move(None, what).wait_send()
     act_move.wait_send()
-    ing_move.wait()
+    for f in range(2):
+        ing_moves[f].wait()
     give(ing_ref, own_ing, irecv)
+
+
+def finish_kernel(
+    act_ref, ing_ref, gr_ref, table_ref, one_ref, two_ref, act_out, ing_out, *outs
+):
+    act_out[...] = act_ref[...]
+    ing_out[...] = ing_ref[...]
+    results = adam(gr_ref[0] + gr_ref[1], table_ref[...], one_ref[...], two_ref[...])
+    for out, result in zip(outs, results):
+        out[...] = result
 
 
 def fused(
@@ -905,6 +920,7 @@
     local = width // 4
     bf, f32 = jnp.bfloat16, jnp.float32
     vmem = pl.BlockSpec(memory_space=pltpu.VMEM)
+    smem = pl.BlockSpec(memory_space=pltpu.SMEM)
     scratch = [
         pltpu.VMEM((4, 3, 2, 2, 2, 96, width), bf),
         pltpu.VMEM((2, 2, 2, 2, 32, width), bf),
@@ -948,8 +964,8 @@
         pltpu.SemaphoreType.DMA((4,)),
         pltpu.SemaphoreType.DMA((13, 9)),
         pltpu.SemaphoreType.DMA((13, 9)),
-        pltpu.SemaphoreType.DMA((4,)),
-        pltpu.SemaphoreType.DMA((4,)),
+        pltpu.SemaphoreType.DMA((5,)),
+        pltpu.SemaphoreType.DMA((5,)),
         pltpu.SemaphoreType.DMA((4,)),
         pltpu.SemaphoreType.DMA((4,)),
         pltpu.SemaphoreType.DMA((4, 4)),
@@ -962,7 +978,7 @@
             jax.ShapeDtypeStruct((shard_rows, micro_count, width), bf),
             jax.ShapeDtypeStruct((2, rank_all, span), f32),
         ),
-        in_specs=[vmem] * 9 + [pl.BlockSpec(memory_space=pltpu.SMEM)],
+        in_specs=[vmem] * 9 + [smem],
         out_specs=(vmem, vmem, vmem),
         scratch_shapes=scratch,
         compiler_params=pltpu.CompilerParams(
@@ -980,9 +996,19 @@
         adapters,
         clip_adapter,
     )
-    return (act.transpose(1, 0, 2), ing.transpose(1, 0, 2)) + adam(
-        grads[0] + grads[1], adapters, moment_one, moment_two
-    )
+    plain = jax.ShapeDtypeStruct((rank_all, span), f32)
+    rows_spec = pl.BlockSpec((shard_rows // 2, micro_count, width), lambda i: (i, 0, 0))
+    plain_spec = pl.BlockSpec((rank_all // 2, span), lambda i: (i, 0))
+    act, ing, *others = pl.pallas_call(
+        finish_kernel,
+        out_shape=(act, ing) + (plain,) * 4 + (jax.ShapeDtypeStruct((rank_all, span), bf),),
+        grid=(2,),
+        in_specs=[rows_spec] * 2
+        + [pl.BlockSpec((2, rank_all // 2, span), lambda i: (0, i, 0))]
+        + [plain_spec] * 3,
+        out_specs=(rows_spec,) * 2 + (plain_spec,) * 5,
+    )(act, ing, grads, adapters, moment_one, moment_two)
+    return (act.transpose(1, 0, 2), ing.transpose(1, 0, 2), *others)
 
 
 def layer(tokens, *others):

time: 121 us -> 118 us (0.975)
  local copies, waits for them, and re-layouts: 2.12 us -> 0 us
  other arithmetic: 2.03 us -> 0 us
    pallas_call x0 -> x1, Pallas kernels: none -> 2.61 us  [fused(): pl.pallas_call(finish_kernel, out_shape=(act, ing) + (plain,) * 4 + (jax....]
    unnamed x12 -> x0, local copies, waits for them, and re-layouts: 2.12 us -> none
    convert_element_type x1 -> x0, other arithmetic: 2.03 us -> none  [adam(): updated.astype(jnp.bfloat16)]
    pallas_call x1, Pallas kernels: 116 us -> 115 us  [fused(): pl.pallas_call(fused_kernel, out_shape=(jax.ShapeDtypeStruct((shard_rows,...]
where the time goes in v4:
time: 118 us
  Pallas kernels  117 us (99%)
    pallas_call x1, Pallas kernels, fused(): pl.pallas_call(fused_kernel, out_shape=(jax.ShapeDtypeStruct((shard_rows,...  115 us
    pallas_call x1, Pallas kernels, fused(): pl.pallas_call(finish_kernel, out_shape=(act, ing) + (plain,) * 4 + (jax....  2.61 us

profile of v4, /device:TPU:0, one launch (start us, length us, event | category | flops | bytes accessed | tf_op | source)
XLA Modules:
  0.0 118.1 jit_solution(7295792351281497925)
XLA Ops:
  0.6 114.7 %shard_map.171 = (bf16[98,4,768]{2,1,0:T(4,128)(2,1)}, bf16[98,4,768]{2,1,0:T(4,128)(2,1)}, f32[2,128,384]{2,1,0:T(8,128)}) custom-call(bf16[98,4,768]{2,1,0:T(4,128)(2,1)} %bitcast.6, bf16[98,4,768]{2,1,0:T(4,128)(2,1)} %bitcast.7, f32[768]{0:T(1024)} %g1_ref.1, f32[768]{0:T(1024)} %g2_ref.1, bf16[3,96,192]{2,1,0:T(8,128)(2,1)} %bitcast.8, ...), custom_call_target="tpu_custom_call" | custom-call | tf_op jit(solution)/shard_map/pallas_call | solution.py:974
  115.3 2.6 %shard_map.172 = (bf16[98,4,768]{2,1,0:T(4,128)(2,1)}, bf16[98,4,768]{2,1,0:T(4,128)(2,1)}, f32[128,384]{1,0:T(8,128)}, f32[128,384]{1,0:T(8,128)}, f32[128,384]...) custom-call(bf16[98,4,768]{2,1,0:T(4,128)(2,1)} %get-tuple-element.17.act_ref, ...), custom_call_target="tpu_custom_call" | custom-call | tf_op jit(solution)/shard_map/pallas_call | solution.py:1002

commit v5 on v4

--- a/solution.py
+++ b/solution.py
@@ -458,12 +458,13 @@
     t1(0)
     for j in range(1, 4):
         ad_move(j).start()
-    for j in range(1, 4):
-        z_move(j).start()
+    z_move(1).start()
     w[z, 1, y, x, c] = wu_ref[...]
     t1(4)
     stage(ts, tok_ref)
     tok_move.start()
+    z_move(2).start()
+    z_move(3).start()
     w[z, 2, y, x, c] = wd_ref[...]
     t2(0)
     t1(1)
@@ -480,13 +481,13 @@
     t1(3)
     t3(1)
     t3(None)
-    stage(cs, cot_ref)
-    cot_move.start()
     t2(3)
     t2(4)
     t3(2)
     z_move(8).start()
     z_move(9).start()
+    stage(cs, cot_ref)
+    cot_move.start()
     t1(5)
     t3(3)
     z_move(10).start()
@@ -814,17 +815,15 @@
     qkv_back = lax.fori_loop(0, 4, attention_back, empty)
     smalls[THR_QKV] = low(qkv_back)
 
-    def first_back(at):
+    for f in range(2):
+        at = pl.ds(f * frame_rows, frame_rows)
         grad = acc[at] + dot(smalls[THR_QKV, at], group(0))
         acc[at] = dn[at] + norm_back(xf[at], g1_ref[...].reshape(1, width), grad)
-
-    tiles(first_back)
-    for f in range(2):
         own, other = halves(f)
         isend[f, pl.ds(0, HALF_PITCH)] = acc[other].astype(jnp.bfloat16)
+        if f == 0:
+            ing_moves[0].start()
         own_ing[f] = acc[own].astype(jnp.bfloat16)
-    for f in range(2):
-        ing_moves[f].start()
     group_ref(0)[...] = t_dot(smalls[THR_QKV], n1[...]).astype(jnp.bfloat16)
     parts = [t_dot(smalls[LOW_QKV], dpj[k]).astype(jnp.bfloat16) for k in range(4)]
     for i in range(3):
@@ -834,6 +833,7 @@
         )
     core_move(0).start()
     spread_out(0)
+    ing_moves[1].start()
 
     act_move.wait_recv()
     give(act_ref, own_act, orecv)

time: 118 us -> 114 us (0.966)
  Pallas kernels: 117 us -> 113 us
    pallas_call x1, Pallas kernels: 115 us -> 110 us  [fused(): pl.pallas_call(fused_kernel, out_shape=(jax.ShapeDtypeStruct((shard_rows,...]
where the time goes in v5:
time: 114 us
  Pallas kernels  113 us (99%)
    pallas_call x1, Pallas kernels, fused(): pl.pallas_call(fused_kernel, out_shape=(jax.ShapeDtypeStruct((shard_rows,...  110 us
    pallas_call x1, Pallas kernels, fused(): pl.pallas_call(finish_kernel, out_shape=(act, ing) + (plain,) * 4 + (jax....  2.61 us

profile of v5, /device:TPU:0, one launch (start us, length us, event | category | flops | bytes accessed | tf_op | source)
XLA Modules:
  0.0 113.8 jit_solution(16696164620237550277)
XLA Ops:
  0.6 110.3 %shard_map.171 = (bf16[98,4,768]{2,1,0:T(4,128)(2,1)}, bf16[98,4,768]{2,1,0:T(4,128)(2,1)}, f32[2,128,384]{2,1,0:T(8,128)}) custom-call(bf16[98,4,768]{2,1,0:T(4,128)(2,1)} %bitcast.6, bf16[98,4,768]{2,1,0:T(4,128)(2,1)} %bitcast.7, f32[768]{0:T(1024)} %g1_ref.1, f32[768]{0:T(1024)} %g2_ref.1, bf16[3,96,192]{2,1,0:T(8,128)(2,1)} %bitcast.8, ...), custom_call_target="tpu_custom_call" | custom-call | tf_op jit(solution)/shard_map/pallas_call | solution.py:974
  111.0 2.6 %shard_map.172 = (bf16[98,4,768]{2,1,0:T(4,128)(2,1)}, bf16[98,4,768]{2,1,0:T(4,128)(2,1)}, f32[128,384]{1,0:T(8,128)}, f32[128,384]{1,0:T(8,128)}, f32[128,384]...) custom-call(bf16[98,4,768]{2,1,0:T(4,128)(2,1)} %get-tuple-element.17.act_ref, ...), custom_call_target="tpu_custom_call" | custom-call | tf_op jit(solution)/shard_map/pallas_call | solution.py:1002

commit v6 on v5

--- a/solution.py
+++ b/solution.py
@@ -273,6 +273,8 @@
     buf,
     dbr,
     dpj,
+    lqh,
+    thr,
     bq,
     ao,
     bu,
@@ -579,7 +581,15 @@
         ao[k] = group(4)[:, k * local : (k + 1) * local]
         bu[k] = group(7 + k)
         an[k] = group(11 + k)
-    smalls[0] = low(dot_t(n1[...], group(0)))
+    low_wide = jnp.where(mask, dot_t(n1[...], group(0)), 0.0)
+    smalls[0] = low_wide.astype(jnp.bfloat16)
+    lqh[...] = jnp.zeros_like(lqh)
+    for r in range(2):
+        for f in range(2):
+            first = f * frame_rows + r * HALF_PITCH
+            lqh[r, pl.ds(f * HALF_SLOT, HALF_PITCH)] = low_wide[
+                first : first + HALF_PITCH
+            ].astype(jnp.bfloat16)
     key_pad = (
         lax.rem(lax.broadcasted_iota(jnp.int32, (frame_rows, 1), 0), HALF_PITCH) >= shard_rows
     )
@@ -761,13 +771,14 @@
     for f in range(2):
         own, other = halves(f)
         osend[f, pl.ds(0, HALF_PITCH)] = acc[other].astype(jnp.bfloat16)
-        own_act[f] = acc[own].astype(jnp.bfloat16)
     act_move.start()
     smalls[THR_OUT] = low(dot_t(dbr[...], group(5)))
     group_ref(5)[...] = t_dot(smalls[LOW_OUT], dbr[...]).astype(jnp.bfloat16)
-    for k in range(4):
-        dpj[k, :, 0:local] = jnp.zeros((rows, local), jnp.bfloat16)
-    acc[...] = jnp.zeros_like(acc)
+    for r in range(2):
+        for k in range(4):
+            dpj[r, k, :, 0:local] = jnp.zeros((2 * HALF_SLOT, local), jnp.bfloat16)
+            for f in range(2):
+                dpj[r, k, pl.ds(f * HALF_SLOT + 96, 16)] = jnp.zeros((16, width), jnp.bfloat16)
 
     spread_out(3)
     spread_out(2)
@@ -776,7 +787,8 @@
     )
     core_move(1).start()
 
-    def attention_back(zk, qkv_back):
+    @pl.loop(0, 4)
+    def _(zk):
         block = attn_block(zk)
         d_att = (dot(dbr[...], block[:, :local]) + dot(smalls[THR_OUT], ao[zk])).astype(
             jnp.bfloat16
@@ -803,29 +815,54 @@
                 d_scores = (wide * (d_soft - inner)).astype(jnp.bfloat16)
                 d_keys = dot(d_scores, q) * scale
                 d_queries = t_dot(k, d_scores).T * scale
-                dpj[zk, at, first : first + HEAD] = d_queries.astype(jnp.bfloat16)
-                dpj[zk, at, first + local : first + local + HEAD] = d_keys.astype(jnp.bfloat16)
-                dpj[zk, at, first + 2 * local : first + 2 * local + HEAD] = d_values.astype(
-                    jnp.bfloat16
-                )
-        d_projected = dpj[zk]
-        acc[...] += dot_t(d_projected, block)
-        return qkv_back + dot_t(d_projected, bq[zk])
-
-    qkv_back = lax.fori_loop(0, 4, attention_back, empty)
-    smalls[THR_QKV] = low(qkv_back)
-
-    for f in range(2):
-        at = pl.ds(f * frame_rows, frame_rows)
-        grad = acc[at] + dot(smalls[THR_QKV, at], group(0))
-        acc[at] = dn[at] + norm_back(xf[at], g1_ref[...].reshape(1, width), grad)
-        own, other = halves(f)
-        isend[f, pl.ds(0, HALF_PITCH)] = acc[other].astype(jnp.bfloat16)
-        if f == 0:
-            ing_moves[0].start()
-        own_ing[f] = acc[own].astype(jnp.bfloat16)
+                for r in range(2):
+                    to = pl.ds(f * HALF_SLOT, HALF_PITCH)
+                    cut = slice(r * HALF_PITCH, (r + 1) * HALF_PITCH)
+                    dpj[r, zk, to, first : first + HEAD] = d_queries[cut].astype(jnp.bfloat16)
+                    dpj[r, zk, to, first + local : first + local + HEAD] = d_keys[cut].astype(
+                        jnp.bfloat16
+                    )
+                    dpj[r, zk, to, first + 2 * local : first + 2 * local + HEAD] = d_values[
+                        cut
+                    ].astype(jnp.bfloat16)
+
+    half_rows = 2 * HALF_SLOT
+    half_mask = (
+        lax.broadcasted_iota(jnp.int32, (half_rows, 32), 0) // HALF_SLOT
+        == lax.broadcasted_iota(jnp.int32, (half_rows, 32), 1) // RANK
+    )
+
+    def half_at(f, r):
+        return pl.ds(pl.multiple_of(f * frame_rows + r * HALF_PITCH, 8), HALF_PITCH)
+
+    def half_products(r):
+        grad = dot_t(dpj[r, 0], attn_block(0))
+        back = dot_t(dpj[r, 0], bq[0])
+        for k in range(1, 4):
+            grad = grad + dot_t(dpj[r, k], attn_block(k))
+            back = back + dot_t(dpj[r, k], bq[k])
+        back = jnp.where(half_mask, back, 0.0)
+        for f in range(2):
+            thr[half_at(f, r)] = back[f * HALF_SLOT : f * HALF_SLOT + HALF_PITCH]
+        tmp[0:half_rows] = grad + dot(back.astype(jnp.bfloat16), group(0))
+
+    def half_back(f, r):
+        at = half_at(f, r)
+        grad = tmp[f * HALF_SLOT : f * HALF_SLOT + HALF_PITCH]
+        value = dn[at] + norm_back(xf[at], g1_ref[...].reshape(1, width), grad)
+        return value.astype(jnp.bfloat16)
+
+    half_products(1 - h)
+    isend[0, pl.ds(0, HALF_PITCH)] = half_back(0, 1 - h)
+    ing_moves[0].start()
+    isend[1, pl.ds(0, HALF_PITCH)] = half_back(1, 1 - h)
+    half_products(h)
+    smalls[THR_QKV] = thr[...].astype(jnp.bfloat16)
     group_ref(0)[...] = t_dot(smalls[THR_QKV], n1[...]).astype(jnp.bfloat16)
-    parts = [t_dot(smalls[LOW_QKV], dpj[k]).astype(jnp.bfloat16) for k in range(4)]
+    parts = [
+        (t_dot(lqh[0], dpj[0, k]) + t_dot(lqh[1], dpj[1, k])).astype(jnp.bfloat16)
+        for k in range(4)
+    ]
     for i in range(3):
         first = (1 + i) * local
         group_ref(1 + i)[...] = jnp.concatenate(
@@ -834,7 +871,11 @@
     core_move(0).start()
     spread_out(0)
     ing_moves[1].start()
-
+    own_ing[0] = half_back(0, h)
+    own_ing[1] = half_back(1, h)
+
+    for f in range(2):
+        own_act[f] = acc[halves(f)[0]].astype(jnp.bfloat16)
     act_move.wait_recv()
     give(act_ref, own_act, orecv)
 
@@ -941,7 +982,9 @@
         pltpu.VMEM((rows, width), f32),
         pltpu.VMEM((2, rows, width), bf),
         pltpu.VMEM((rows, width), bf),
-        pltpu.VMEM((4, rows, width), bf),
+        pltpu.VMEM((2, 4, 2 * HALF_SLOT, width), bf),
+        pltpu.VMEM((2, 2 * HALF_SLOT, 32), bf),
+        pltpu.VMEM((rows, 32), f32),
         pltpu.VMEM((4, 32, width), bf),
         pltpu.VMEM((4, 32, local), bf),
         pltpu.VMEM((4, 32, width), bf),

time: 114 us -> 113 us (level)
  no operation moved by 1% of the time
where the time goes in v6:
time: 113 us
  Pallas kernels  112 us (99%)
    pallas_call x1, Pallas kernels, fused(): pl.pallas_call(fused_kernel, out_shape=(jax.ShapeDtypeStruct((shard_rows,...  109 us
    pallas_call x1, Pallas kernels, fused(): pl.pallas_call(finish_kernel, out_shape=(act, ing) + (plain,) * 4 + (jax....  2.61 us

profile of v6, /device:TPU:0, one launch (start us, length us, event | category | flops | bytes accessed | tf_op | source)
XLA Modules:
  0.0 112.9 jit_solution(4957862993917768961)
XLA Ops:
  0.6 109.4 %shard_map.171 = (bf16[98,4,768]{2,1,0:T(4,128)(2,1)}, bf16[98,4,768]{2,1,0:T(4,128)(2,1)}, f32[2,128,384]{2,1,0:T(8,128)}) custom-call(bf16[98,4,768]{2,1,0:T(4,128)(2,1)} %bitcast.6, bf16[98,4,768]{2,1,0:T(4,128)(2,1)} %bitcast.7, f32[768]{0:T(1024)} %g1_ref.1, f32[768]{0:T(1024)} %g2_ref.1, bf16[3,96,192]{2,1,0:T(8,128)(2,1)} %bitcast.8, ...), custom_call_target="tpu_custom_call" | custom-call | tf_op jit(solution)/shard_map/pallas_call | solution.py:1017
  110.1 2.6 %shard_map.172 = (bf16[98,4,768]{2,1,0:T(4,128)(2,1)}, bf16[98,4,768]{2,1,0:T(4,128)(2,1)}, f32[128,384]{1,0:T(8,128)}, f32[128,384]{1,0:T(8,128)}, f32[128,384]...) custom-call(bf16[98,4,768]{2,1,0:T(4,128)(2,1)} %get-tuple-element.17.act_ref, ...), custom_call_target="tpu_custom_call" | custom-call | tf_op jit(solution)/shard_map/pallas_call | solution.py:1045

commit v7 on v6

--- a/solution.py
+++ b/solution.py
@@ -669,6 +669,10 @@
             t1(q + 3)
             t2(q + 2)
 
+        @pl.when(i > 0)
+        def _():
+            ready(q)
+
         tmp[...] = dot(n2[...], w[zk, 1].reshape(width, width)) + dot(smalls[LOW_UP], bu[zk])
 
         def gate(at):
@@ -714,7 +718,6 @@
         @pl.when(i < 3)
         def _():
             t3(q + 2)
-            ready(q + 2)
 
         return down_low, up_back
 
@@ -835,7 +838,7 @@
     def half_at(f, r):
         return pl.ds(pl.multiple_of(f * frame_rows + r * HALF_PITCH, 8), HALF_PITCH)
 
-    def half_products(r):
+    def half_products(r, out):
         grad = dot_t(dpj[r, 0], attn_block(0))
         back = dot_t(dpj[r, 0], bq[0])
         for k in range(1, 4):
@@ -844,19 +847,18 @@
         back = jnp.where(half_mask, back, 0.0)
         for f in range(2):
             thr[half_at(f, r)] = back[f * HALF_SLOT : f * HALF_SLOT + HALF_PITCH]
-        tmp[0:half_rows] = grad + dot(back.astype(jnp.bfloat16), group(0))
-
-    def half_back(f, r):
+        out[0:half_rows] = grad + dot(back.astype(jnp.bfloat16), group(0))
+
+    def half_back(f, r, products):
         at = half_at(f, r)
-        grad = tmp[f * HALF_SLOT : f * HALF_SLOT + HALF_PITCH]
+        grad = products[f * HALF_SLOT : f * HALF_SLOT + HALF_PITCH]
         value = dn[at] + norm_back(xf[at], g1_ref[...].reshape(1, width), grad)
         return value.astype(jnp.bfloat16)
 
-    half_products(1 - h)
-    isend[0, pl.ds(0, HALF_PITCH)] = half_back(0, 1 - h)
+    half_products(1 - h, tmp)
+    isend[0, pl.ds(0, HALF_PITCH)] = half_back(0, 1 - h, tmp)
     ing_moves[0].start()
-    isend[1, pl.ds(0, HALF_PITCH)] = half_back(1, 1 - h)
-    half_products(h)
+    half_products(h, mid)
     smalls[THR_QKV] = thr[...].astype(jnp.bfloat16)
     group_ref(0)[...] = t_dot(smalls[THR_QKV], n1[...]).astype(jnp.bfloat16)
     parts = [
@@ -869,10 +871,11 @@
             [parts[k][:, first : first + local] for k in range(4)], axis=1
         )
     core_move(0).start()
+    isend[1, pl.ds(0, HALF_PITCH)] = half_back(1, 1 - h, tmp)
     spread_out(0)
     ing_moves[1].start()
-    own_ing[0] = half_back(0, h)
-    own_ing[1] = half_back(1, h)
+    own_ing[0] = half_back(0, h, mid)
+    own_ing[1] = half_back(1, h, mid)
 
     for f in range(2):
         own_act[f] = acc[halves(f)[0]].astype(jnp.bfloat16)

time: 113 us -> 113 us (level)
  no operation moved by 1% of the time
where the time goes in v7:
time: 113 us; the launch traced here: 112 us
  Pallas kernels  112 us (99%)
    pallas_call x1, Pallas kernels, fused(): pl.pallas_call(fused_kernel, out_shape=(jax.ShapeDtypeStruct((shard_rows,...  109 us
    pallas_call x1, Pallas kernels, fused(): pl.pallas_call(finish_kernel, out_shape=(act, ing) + (plain,) * 4 + (jax....  2.61 us

profile of v7, /device:TPU:0, one launch (start us, length us, event | category | flops | bytes accessed | tf_op | source)
XLA Modules:
  0.0 112.4 jit_solution(4862661575966919056)
XLA Ops:
  0.6 108.9 %shard_map.171 = (bf16[98,4,768]{2,1,0:T(4,128)(2,1)}, bf16[98,4,768]{2,1,0:T(4,128)(2,1)}, f32[2,128,384]{2,1,0:T(8,128)}) custom-call(bf16[98,4,768]{2,1,0:T(4,128)(2,1)} %bitcast.6, bf16[98,4,768]{2,1,0:T(4,128)(2,1)} %bitcast.7, f32[768]{0:T(1024)} %g1_ref.1, f32[768]{0:T(1024)} %g2_ref.1, bf16[3,96,192]{2,1,0:T(8,128)(2,1)} %bitcast.8, ...), custom_call_target="tpu_custom_call" | custom-call | tf_op jit(solution)/shard_map/pallas_call | solution.py:1020
  109.6 2.6 %shard_map.172 = (bf16[98,4,768]{2,1,0:T(4,128)(2,1)}, bf16[98,4,768]{2,1,0:T(4,128)(2,1)}, f32[128,384]{1,0:T(8,128)}, f32[128,384]{1,0:T(8,128)}, f32[128,384]...) custom-call(bf16[98,4,768]{2,1,0:T(4,128)(2,1)} %get-tuple-element.17.act_ref, ...), custom_call_target="tpu_custom_call" | custom-call | tf_op jit(solution)/shard_map/pallas_call | solution.py:1048

commit v8 on v7

--- a/solution.py
+++ b/solution.py
@@ -571,8 +571,6 @@
     tiles(first_norm)
     ready(None)
     for k in range(4):
-        ready(k)
-    for k in range(4):
         bq[k] = jnp.concatenate(
             [jnp.zeros((32, local), jnp.bfloat16)]
             + [group(1 + i)[:, k * local : (k + 1) * local] for i in range(3)],
@@ -634,6 +632,12 @@
         def _():
             t1(7)
             t2(6)
+
+        for k in range(4):
+
+            @pl.when(i == k)
+            def _():
+                ready(k)
 
         return attention(i, out_low)
 

time: 113 us -> 111 us (0.982)
  Pallas kernels: 112 us -> 110 us
    pallas_call x1, Pallas kernels: 109 us -> 107 us  [fused(): pl.pallas_call(fused_kernel, out_shape=(jax.ShapeDtypeStruct((shard_rows,...]
where the time goes in v8:
time: 111 us
  Pallas kernels  110 us (99%)
    pallas_call x1, Pallas kernels, fused(): pl.pallas_call(fused_kernel, out_shape=(jax.ShapeDtypeStruct((shard_rows,...  107 us
    pallas_call x1, Pallas kernels, fused(): pl.pallas_call(finish_kernel, out_shape=(act, ing) + (plain,) * 4 + (jax....  2.61 us

profile of v8, /device:TPU:0, one launch (start us, length us, event | category | flops | bytes accessed | tf_op | source)
XLA Modules:
  0.0 110.9 jit_solution(4941418688413978642)
XLA Ops:
  0.6 107.5 %shard_map.171 = (bf16[98,4,768]{2,1,0:T(4,128)(2,1)}, bf16[98,4,768]{2,1,0:T(4,128)(2,1)}, f32[2,128,384]{2,1,0:T(8,128)}) custom-call(bf16[98,4,768]{2,1,0:T(4,128)(2,1)} %bitcast.6, bf16[98,4,768]{2,1,0:T(4,128)(2,1)} %bitcast.7, f32[768]{0:T(1024)} %g1_ref.1, f32[768]{0:T(1024)} %g2_ref.1, bf16[3,96,192]{2,1,0:T(8,128)(2,1)} %bitcast.8, ...), custom_call_target="tpu_custom_call" | custom-call | tf_op jit(solution)/shard_map/pallas_call | solution.py:1024
  108.1 2.6 %shard_map.172 = (bf16[98,4,768]{2,1,0:T(4,128)(2,1)}, bf16[98,4,768]{2,1,0:T(4,128)(2,1)}, f32[128,384]{1,0:T(8,128)}, f32[128,384]{1,0:T(8,128)}, f32[128,384]...) custom-call(bf16[98,4,768]{2,1,0:T(4,128)(2,1)} %get-tuple-element.17.act_ref, ...), custom_call_target="tpu_custom_call" | custom-call | tf_op jit(solution)/shard_map/pallas_call | solution.py:1052

commit v9 on v8

--- a/solution.py
+++ b/solution.py
@@ -488,8 +488,6 @@
     t3(2)
     z_move(8).start()
     z_move(9).start()
-    stage(cs, cot_ref)
-    cot_move.start()
     t1(5)
     t3(3)
     z_move(10).start()
@@ -619,6 +617,11 @@
         return out_low + dot_t(gathered, ao[zk])
 
     def attention_step(i, out_low):
+        @pl.when(i == 0)
+        def _():
+            stage(cs, cot_ref)
+            cot_move.start()
+
         @pl.when(i == 1)
         def _():
             t1(6)

time: 111 us -> 114 us (1.027)
  Pallas kernels: 110 us -> 113 us
    pallas_call x1, Pallas kernels: 107 us -> 110 us  [fused(): pl.pallas_call(fused_kernel, out_shape=(jax.ShapeDtypeStruct((shard_rows,...]
where the time goes in v9:
time: 114 us
  Pallas kernels  113 us (99%)
    pallas_call x1, Pallas kernels, fused(): pl.pallas_call(fused_kernel, out_shape=(jax.ShapeDtypeStruct((shard_rows,...  110 us
    pallas_call x1, Pallas kernels, fused(): pl.pallas_call(finish_kernel, out_shape=(act, ing) + (plain,) * 4 + (jax....  2.61 us

profile of v9, /device:TPU:0, one launch (start us, length us, event | category | flops | bytes accessed | tf_op | source)
XLA Modules:
  0.0 113.8 jit_solution(13604225377873870599)
XLA Ops:
  0.6 110.3 %shard_map.171 = (bf16[98,4,768]{2,1,0:T(4,128)(2,1)}, bf16[98,4,768]{2,1,0:T(4,128)(2,1)}, f32[2,128,384]{2,1,0:T(8,128)}) custom-call(bf16[98,4,768]{2,1,0:T(4,128)(2,1)} %bitcast.6, bf16[98,4,768]{2,1,0:T(4,128)(2,1)} %bitcast.7, f32[768]{0:T(1024)} %g1_ref.1, f32[768]{0:T(1024)} %g2_ref.1, bf16[3,96,192]{2,1,0:T(8,128)(2,1)} %bitcast.8, ...), custom_call_target="tpu_custom_call" | custom-call | tf_op jit(solution)/shard_map/pallas_call | solution.py:1027
  111.0 2.6 %shard_map.172 = (bf16[98,4,768]{2,1,0:T(4,128)(2,1)}, bf16[98,4,768]{2,1,0:T(4,128)(2,1)}, f32[128,384]{1,0:T(8,128)}, f32[128,384]{1,0:T(8,128)}, f32[128,384]...) custom-call(bf16[98,4,768]{2,1,0:T(4,128)(2,1)} %get-tuple-element.17.act_ref, ...), custom_call_target="tpu_custom_call" | custom-call | tf_op jit(solution)/shard_map/pallas_call | solution.py:1055
